TPU v7x, 32 devices: a whole 2x2x4 slice. The times are simulated.
32 devices in a mesh: dp: 8 (over y, x, core), mp: 4 (over z).
Axes of the slice: x: 2, y: 2, z: 4, core: 2. Of those that a mesh axis runs over, the one named last changes fastest.
Arguments:
- tokens_in: bfloat16 [192, 196, 384], P(('dp', 'mp')), may hold values from -6 to 6
- image_counts: int32 [8], P('dp'), may hold values from 1 to 24, as said below
- norm1_gain: float32 [384], replicated, may hold values from 0.25 to 1.75
- norm1_bias: float32 [384], replicated, may hold values from -1.75 to 1.75
- qkv_weight: bfloat16 [384, 1152], replicated, may hold values from -0.3125 to 0.3125
- qkv_bias: float32 [1152], replicated, may hold values from -1.75 to 1.75
- mix_pre: float32 [8, 8], replicated, may hold values from -3 to 3
- mix_post: float32 [8, 8], replicated, may hold values from -2 to 2
- mix_post_bias: float32 [8], replicated, may hold values from -0.0625 to 0.0625
- proj_weight: bfloat16 [384, 384], replicated, may hold values from -2 to 2
- proj_bias: float32 [384], replicated, may hold values from -1.75 to 1.75
- gamma1: float32 [384], replicated, may hold values from 0.25 to 1.75
- norm2_gain: float32 [384], replicated, may hold values from 0.25 to 1.75
- norm2_bias: float32 [384], replicated, may hold values from -1.75 to 1.75
- fc1_weight: bfloat16 [384, 1536], P(None, 'mp'), may hold values from -0.3125 to 0.3125
- fc1_bias: float32 [1536], P('mp'), may hold values from -1.75 to 1.75
- fc2_weight: bfloat16 [1536, 384], P('mp'), may hold values from -0.15625 to 0.15625
- fc2_bias: float32 [384], replicated, may hold values from -1.75 to 1.75
- gamma2: float32 [384], replicated, may hold values from 0.25 to 1.75
- out_grad: bfloat16 [192, 196, 384], P(('dp', 'mp')), may hold values from -6 to 6
Outputs:
- layer_out: bfloat16 [192, 196, 384], P(('dp', 'mp'))
- in_grad: float32 [192, 196, 384], P(('dp', 'mp'))
- grad_norm1_gain: float32 [384], P('dp')
- grad_norm1_bias: float32 [384], P('dp')
- grad_qkv_weight: float32 [384, 1152], P(None, 'dp')
- grad_qkv_bias: float32 [1152], P('dp')
- grad_mix_pre: float32 [8, 8], replicated
- grad_mix_post: float32 [8, 8], replicated
- grad_mix_post_bias: float32 [8], replicated
- grad_proj_weight: float32 [384, 384], P(None, 'dp')
- grad_proj_bias: float32 [384], P('dp')
- grad_gamma1: float32 [384], P('dp')
- grad_norm2_gain: float32 [384], P('dp')
- grad_norm2_bias: float32 [384], P('dp')
- grad_fc1_weight: float32 [384, 1536], P(None, ('mp', 'dp'))
- grad_fc1_bias: float32 [1536], P(('mp', 'dp'))
- grad_fc2_weight: float32 [1536, 384], P('mp', 'dp')
- grad_fc2_bias: float32 [384], P('dp')
- grad_gamma2: float32 [384], P('dp')
Inputs may be any that keep to these rules, and one draw needn't show every extreme that they name: image_counts[g] images of data group g are present, filling its first slots; some group holds all 24.
All inputs are finite; a program needn't handle non-finite values.
Results may differ from a plain program's by a relative error of at most 0.015.
The roundings to bfloat16 on the way count: a program that leaves them out, or rounds other values in their place, can miss the bound.
Values may be sent and summed in bfloat16 or wider, within the bound.
No kernel may reach another device: no remote copies, remote signals or barrier semaphores. Data moves between devices by JAX's collectives and lax.ppermute only.
A program may use at most 192 MiB of HBM per device.

v0:
```python
import functools

import jax
import jax.numpy as jnp
from jax import lax
from jax.experimental import pallas as pl
from jax.experimental.pallas import tpu as pltpu
from jax.sharding import PartitionSpec as P

BF = jnp.bfloat16
F32 = jnp.float32
EPS = 1e-06
VMEM_LIMIT = 20 * 1024 * 1024


def nn(a, b):
    return lax.dot_general(a, b, (((1,), (0,)), ((), ())), preferred_element_type=F32)


def nt(a, b):
    return lax.dot_general(a, b, (((1,), (1,)), ((), ())), preferred_element_type=F32)


def tn(a, b):
    return lax.dot_general(a, b, (((0,), (0,)), ((), ())), preferred_element_type=F32)


def exact(a, b, dims):
    return lax.dot_general(
        a, b, (dims, ((), ())), precision=lax.Precision.HIGHEST, preferred_element_type=F32
    )


def normalized(x):
    mean = jnp.mean(x, axis=-1, keepdims=True)
    c = x - mean
    r = lax.rsqrt(jnp.mean(c * c, axis=-1, keepdims=True) + EPS)
    return c * r, r


def norm_back(cot, n, r, gain):
    cg = cot * gain
    return r * (
        cg
        - jnp.mean(cg, axis=-1, keepdims=True)
        - n * jnp.mean(cg * n, axis=-1, keepdims=True)
    )


def colsum(x):
    return jnp.sum(x, axis=0, keepdims=True)


def split(x):
    hi = x.astype(BF)
    return jnp.concatenate([hi, (x - hi.astype(F32)).astype(BF)], axis=1)


def row(ref):
    return ref[...].reshape(1, ref.shape[0])


def gelu_parts(z):
    e = jnp.exp(z * z * -0.5)
    t = pl.reciprocal(1.0 + jnp.abs(z) * (0.3275911 * 0.7071067811865476), approx=True)
    poly = t * (
        0.5 * 0.254829592
        + t
        * (
            0.5 * -0.284496736
            + t * (0.5 * 1.421413741 + t * (0.5 * -1.453152027 + t * (0.5 * 1.061405429)))
        )
    )
    tail = poly * e
    phi = jnp.where(z >= 0, 1.0 - tail, tail)
    return phi, phi + z * e * 0.3989422804014327


def head_of_lane(shape, axis, head_dim):
    return lax.broadcasted_iota(jnp.int32, shape, axis) // head_dim


def chunks(count, size=16):
    return [slice(at, at + size) for at in range(0, count, size)]


def fold(x):
    return sum(x[at : at + 8] for at in range(8, x.shape[0], 8)) + x[0:8]


def pack_kernel(w1, w2, b1, *refs):
    many = (len(refs) - 3) // 2
    sources, other, held, b1_v, sems = refs[:many], refs[many], refs[many + 1 : -2], refs[-2], refs[-1]
    feats = w1.shape[0]
    core = jnp.bitwise_and(lax.axis_index("dp"), 1)
    bias_copy = pltpu.make_async_copy(b1, b1_v, sems.at[0])
    own = [pltpu.make_async_copy(w, other.at[0:feats], sems.at[1]) for w in (w1, w2)]
    copies = [
        pltpu.make_async_copy(sources[j], held[j], sems.at[2 + j]) for j in range(many)
    ]
    bias_copy.start()
    for j in range(2):
        pl.when(core == j)(own[j].start)
    for copy in copies:
        copy.start()
    bias_copy.wait()
    rest = row(b1_v)
    place = lax.broadcasted_iota(jnp.int32, (16, feats), 0)
    bias = jnp.zeros((16, feats), F32)
    for j in range(3):
        term = rest.astype(BF).astype(F32)
        bias = jnp.where(place == j, term, bias)
        rest = rest - term
    other[feats:, :] = bias.astype(BF)
    for j in range(2):
        pl.when(core == j)(own[j].wait)
    for copy in copies:
        copy.wait()


def attn_fwd_kernel(first, share, *refs):
    counts, post_s, postb_s, tok, og, n1g, n1b, qkvb, pre, post, postb, projb = refs[:12]
    gamma1, n2g, n2b, wqkv, wproj = refs[12:17]
    a1_o, q_o, k_o, v_o, p_o, o_o, x1_o, u_o, a2_o, dy_o, mpre, mpost, mixb = refs[-19:-6]
    pad, kk, attended_t, wide, logits, mixed = refs[-6:]
    images, patches, feats = tok.shape
    rows = pad.shape[0]
    heads = mpre.shape[0]
    head_dim = feats // heads
    slots = q_o.shape[1]

    spread = (
        head_of_lane((heads, feats), 1, head_dim)
        == lax.broadcasted_iota(jnp.int32, (heads, feats), 0)
    ).astype(F32)
    mpre[...] = exact(pre[...], spread, ((1,), (0,))) * head_dim**-0.5
    mpost[...] = exact(post[...], spread, ((0,), (0,)))
    mixb[...] = exact(row(postb), spread, ((1,), (0,)))

    @pl.loop(first, first + share)
    def _(i):
        pad[patches:, :] = jnp.zeros((rows - patches, feats), F32)
        live = (lax.axis_index("mp") * images + i < counts[0]).astype(F32)
        pad[0:patches, :] = og[i].astype(F32) * live
        dy_o[i] = pad[...].astype(BF)
        pad[0:patches, :] = tok[i].astype(F32)
        gain, shift = row(n1g), row(n1b)
        for c in chunks(rows):
            n, _ = normalized(pad[c, :])
            a1_o[i, c, :] = (n * gain + shift).astype(BF)
        wide[...] = nn(a1_o[i], wqkv[...])
        bias = row(qkvb)
        q_o[i, rows:] = jnp.zeros((slots - rows, feats), BF)
        for c in chunks(rows):
            q, k, v = (
                wide[c, j * feats : (j + 1) * feats] + bias[:, j * feats : (j + 1) * feats]
                for j in range(3)
            )
            q_o[i, c, :] = q.astype(BF)
            v_o[i, c, :] = v.astype(BF)
            k = k.astype(BF)
            k_o[i, c, :] = k
            kf = k.astype(F32)
            for g in range(heads):
                at = slice(g * rows + c.start, g * rows + c.stop)
                scaled = kf * mpre[g : g + 1, :]
                hi = scaled.astype(BF)
                kk[at, 0:feats] = hi
                kk[at, feats:] = (scaled - hi.astype(F32)).astype(BF)
        q2 = jnp.concatenate([q_o[i], q_o[i]], axis=1)
        vt = v_o[i].T
        many = heads // 2
        half = many * rows
        tail = patches // 8 * 8
        inside = lax.broadcasted_iota(jnp.int32, (rows - tail, 128), 0) < patches - tail
        real = (lax.broadcasted_iota(jnp.int32, (rows, 128), 0) < patches).astype(BF)
        start = nn(vt, real)
        for s in range(2):
            part = slice(s * half, (s + 1) * half)
            logits[part, :] = nt(kk[part, :], q2)
        for g in range(heads):
            for lane in range(0, slots, 128):
                x = logits[g * rows : (g + 1) * rows, lane : lane + 128]
                x = jnp.concatenate([x[0:tail], jnp.where(inside, x[tail:], -1e30)], axis=0)
                e = jnp.exp(x - jnp.max(x, axis=0, keepdims=True))
                inv = 1.0 / jnp.sum(e, axis=0, keepdims=True)
                p_o[i, g, :, lane : lane + 128] = (e * inv).astype(BF)
            mixed[g] = nn(vt, p_o[i, g])
        for c in chunks(feats):
            g = c.start // head_dim
            first = start[c] * postb_s[g]
            for lane in range(0, slots, 128):
                total = first
                for h in range(heads):
                    total = total + mixed[h, c, lane : lane + 128] * post_s[g, h]
                attended_t[c, lane : lane + 128] = total.astype(BF)
        o_o[i] = attended_t[...].T[0:rows]
        wide[:, 0:feats] = nn(o_o[i], wproj[...])
        bias, scale, gain, shift = row(projb), row(gamma1), row(n2g), row(n2b)
        for c in chunks(rows):
            u = wide[c, 0:feats] + bias
            x1 = pad[c, :] + scale * u
            u_o[i, c, :] = u
            x1_o[i, c, :] = x1
            n, _ = normalized(x1)
            a2_o[i, c, :] = (n * gain + shift).astype(BF)


def store_blocks(count, put):
    mine = lax.axis_index("dp")
    for core in range(2):

        @pl.when(jnp.bitwise_and(mine, 1) == core)
        def _(core=core):
            for b in range(count):
                place = jnp.bitwise_xor(jnp.int32(b >> 1), jnp.right_shift(mine, 1))
                put((b ^ core) & 1, place, b)


def mlp_units(a2, dfs, w1, b1, w2, hids, dzs, zs, ghs, units, store, use):
    size = a2.shape[0] // units
    width = w2.shape[0]
    lanes = zs.shape[2]
    places = [slice(u * size, (u + 1) * size) for u in range(units)]
    blocks = [(u, at) for u in range(units) for at in range(0, width, lanes)]

    def products(j):
        u, at = blocks[j]
        part = slice(at, at + lanes)
        zs[j % 2] = nn(a2[places[u], :], w1[:, part])
        ghs[j % 2] = nt(dfs[places[u], :], w2[part, :])

    def activation(j):
        u, at = blocks[j]
        part = slice(at, at + lanes)
        bias = b1[:, part]
        for c in chunks(size):
            zc = zs[j % 2, c, :] + bias
            phi, slope = gelu_parts(zc)
            rows = slice(places[u].start + c.start, places[u].start + c.stop)
            hids[rows, part] = (zc * phi).astype(BF)
            dzs[rows, part] = (ghs[j % 2, c, :] * slope).astype(BF)

    def finish(u):
        store(places[u], nn(hids[places[u], :], w2[...]), nt(dzs[places[u], :], w1[...]))

    products(0)
    for j, (u, at) in enumerate(blocks):
        if j + 1 < len(blocks):
            products(j + 1)
        if at == lanes and u > 0:
            finish(u - 1)
        activation(j)
        if at == 2 * lanes and u > 0:
            use(places[u - 1])
    finish(units - 1)
    use(places[units - 1])


def mlp_first_kernel(
    a2, dy, gamma2, w1_own, b1_own, w2_own, near, far,
    f_o, da2_o, hids, dzs, dfs,
    w1, w2, b1, zs, ghs,
):
    total, feats = f_o.shape
    w1[:, 0:feats] = w1_own[...]
    w2[0:feats, :] = w2_own[...]
    for core in range(2):

        @pl.when(jnp.bitwise_and(lax.axis_index("dp"), 1) == core)
        def _(core=core):
            one, two = (near, far) if core == 0 else (far, near)
            w1[:, feats:] = one[0, 0:feats]
            w2[feats:, :] = two[0, 0:feats]

    b1[:, 0:feats] = row(b1_own)
    b1[:, feats:] = colsum(near[0, feats : feats + 16].astype(F32))
    gain = row(gamma2)
    for c in chunks(total):
        dfs[c, :] = (dy[c, :].astype(F32) * gain).astype(BF)

    def store(rows, f, da2):
        f_o[rows, :] = f
        da2_o[rows, :] = da2

    mlp_units(a2, dfs, w1, b1, w2, hids, dzs, zs, ghs, 3, store, lambda rows: None)


def mlp_grad_kernel(a2, hids, dzs, dfs, grads, b1_o, a2t, dft):
    feats = a2.shape[1]
    a2t[0:feats, :] = a2[...].T
    a2t[feats:, :] = jnp.ones((a2t.shape[0] - feats, a2t.shape[1]), BF)
    dft[...] = dfs[...].T
    up = nn(a2t[...], dzs[...])
    b1_o[...] = up[feats : feats + 1]
    grads[0] = up[0:feats].astype(BF).T
    down = nn(dft[...], hids[...]).astype(BF)
    for c in range(2):
        grads[1, c * feats : (c + 1) * feats, :] = down[:, c * feats : (c + 1) * feats]


def mlp_rest_kernel(
    counts, a2, dy, dfs, x1, u, o, f0, da20, near, far, last, far_last, grads, a2t, dft, wproj,
    gamma1, n2g, fc2b, gamma2,
    out_o, dx1_o, do_o, keep, send, b1_o, acc_o,
    w1, w2, b1, hids, dzs, zs, ghs, fs, da2s, dus, ups, downs, projs, out_v, sems,
):
    total, feats = f0.shape
    images, patches = out_o.shape[:2]
    image_rows = total // images
    m_idx = lax.axis_index("mp")
    acc_o[...] = jnp.zeros_like(acc_o)
    b1[:, 0:feats] = colsum(near[1, feats : feats + 16].astype(F32))
    b1[:, feats:] = colsum(last[feats : feats + 16].astype(F32))
    for core in range(2):

        @pl.when(jnp.bitwise_and(lax.axis_index("dp"), 1) == core)
        def _(core=core):
            one, two = (near, far) if core == 0 else (far, near)
            w1[:, 0:feats] = one[1, 0:feats]
            w2[0:feats, :] = two[1, 0:feats]
            one, two = (last, far_last) if core == 0 else (far_last, last)
            w1[:, feats:] = one[0:feats]
            w2[feats:, :] = two[0:feats]

    gain2 = row(gamma2)
    bias, gain, scale = row(fc2b), row(n2g), row(gamma1)

    def out_copy(image):
        return pltpu.make_async_copy(out_v.at[image], out_o.at[image], sems.at[image])

    def store(rows, f, da2):
        fs[rows, :] = f
        da2s[rows, :] = da2

    def use(rows):
        sums = [jnp.zeros((8, feats), F32) for _ in range(6)]
        for c in chunks(rows.stop - rows.start):
            at = slice(rows.start + c.start, rows.start + c.stop)
            fc = fs[at, :] + f0[at, :] + bias
            dac = da2s[at, :] + da20[at, :]
            x1c = x1[at, :]
            dyc = dy[at, :].astype(F32)
            n, r = normalized(x1c)
            dx1 = dyc + norm_back(dac, n, r, gain)
            dx1_o[at, :] = dx1
            du = (dx1 * scale).astype(BF)
            dus[at, :] = du
            image = at.start // image_rows
            first = at.start - image * image_rows
            live = (m_idx * images + image < counts[0]).astype(F32)
            out = ((x1c + gain2 * fc) * live).astype(BF)
            if first + 16 <= patches:
                out_v[image, first : first + 16, :] = out
            else:
                out_v[image, first:patches, :] = out[0 : patches - first]
            terms = (
                du.astype(F32), u[at, :] * dx1, dac * n, dac, dfs[at, :].astype(F32), fc * dyc,
            )
            sums = [s + fold(t) for s, t in zip(sums, terms)]
        for j in range(6):
            acc_o[j : j + 1, :] += colsum(sums[j])
        do = nt(dus[rows, :], wproj[...]).astype(BF)
        for at in range(0, rows.stop - rows.start, image_rows):
            image = (rows.start + at) // image_rows
            out_copy(image).start()
            do_o[image, 0:image_rows] = do[at : at + image_rows]
            do_o[image, image_rows:] = jnp.zeros((do_o.shape[1] - image_rows, feats), BF)

    mlp_units(a2, dfs, w1, b1, w2, hids, dzs, zs, ghs, 3, store, use)
    up = nn(a2t[...], dzs[...])
    b1_o[...] = up[feats : feats + 1]
    ups[...] = up[0:feats].astype(BF).T
    downs[...] = nn(dft[...], hids[...]).astype(BF)
    projs[...] = tn(dus[...], o[...]).astype(BF)
    count = 2 * keep.shape[0]
    size = feats // count
    outs = (keep, send)

    def put(which, place, b):
        out = outs[which]
        for c in range(2):
            part = slice(c * feats, (c + 1) * feats)
            up = slice(c * feats + b * size, c * feats + (b + 1) * size)
            down = slice(b * size, (b + 1) * size)
            pieces = (grads[0, up, :], grads[1, up, :])
            for j, piece in enumerate(pieces):
                out[place, (2 * c + j) * size : (2 * c + j + 1) * size, :] = piece
            pieces = (ups[up, :], downs[down, part])
            for j, piece in enumerate(pieces):
                out[place, (4 + 2 * c + j) * size : (5 + 2 * c + j) * size, :] = piece
        out[place, 8 * size : 9 * size, :] = projs[b * size : (b + 1) * size, :]

    store_blocks(count, put)
    for image in range(images):
        out_copy(image).wait()


def attn_bwd_kernel(first, share, *refs):
    pre_s, do_r, q_r, k_r, v_r, p_r, dx1, tok, mpre, mpost, mixb, wqkv, n1g = refs[:13]
    if first:
        before, in_o = refs[14], refs[-13]
        dqkv_o, acc_o = refs[-14], refs[-12]
        vgs, dls, dq_t, dps, dvs, dks, dqs, da1, pad, in_v, sems = refs[-11:]
    else:
        dqkv_o, in_v, acc_o, vgs, dls, dq_t, dps, dvs, dks, dqs, da1, pad = refs[-12:]
    slots, feats = do_r.shape[1:]
    patches = tok.shape[1]
    rows = k_r.shape[1]
    heads = mpre.shape[0]
    head_dim = feats // heads
    acc_o[...] = jnp.zeros_like(acc_o)

    def in_copy(i):
        return pltpu.make_async_copy(in_v.at[i - first], in_o.at[i], sems.at[i])

    def early_copy(i):
        return pltpu.make_async_copy(before.at[i], in_o.at[i], sems.at[i])

    for i in range(first):
        early_copy(i).start()

    @pl.loop(first, first + share)
    def _(i):
        do_sum = jnp.zeros((8, feats), F32)
        for c in chunks(rows):
            do_sum = do_sum + fold(do_r[i, c, :].astype(F32))
        do_sum = colsum(do_sum)
        q = q_r[i]
        do = do_r[i]
        kt = k_r[i].T

        def products(pair):
            for c in chunks(rows):
                vf = v_r[i, c, :].astype(F32)
                for h in pair:
                    at = slice(h * rows + c.start, h * rows + c.stop)
                    vgs[at, :] = (vf * mpost[h : h + 1, :]).astype(BF)
            part = slice(pair[0] * rows, (pair[1] + 1) * rows)
            dps[part, :] = nt(vgs[part, :], do)
            dvs[part, :] = nn(p_r[i, pair[0] : pair[1] + 1].reshape(2 * rows, slots), do)

        products((0, 1))
        for h in range(heads):
            if h % 2 == 0 and h + 2 < heads:
                products((h + 2, h + 3))
            at = slice(h * rows, (h + 1) * rows)
            for lane in range(0, slots, 128):
                dp = dps[at, lane : lane + 128]
                pf = p_r[i, h, :, lane : lane + 128].astype(F32)
                mean = jnp.sum(dp * pf, axis=0, keepdims=True) / jnp.sum(
                    pf, axis=0, keepdims=True
                )
                dls[at, lane : lane + 128] = (pf * (dp - mean)).astype(BF)
            dqs[h] = nn(kt, dls[at, :])
            if h % 2 == 1:
                part = slice((h - 1) * rows, (h + 1) * rows)
                dks[part, :] = nn(dls[part, :], q)

        bias_row = mixb[...] * do_sum
        v_sum = jnp.zeros((8, feats), F32)
        dv_sum = jnp.zeros((8, feats), F32)
        sums = [jnp.zeros((8, feats), F32) for _ in range(heads)]
        for c in chunks(rows):
            vf = v_r[i, c, :].astype(F32)
            dv = bias_row
            for h in range(heads):
                this = dvs[h * rows + c.start : h * rows + c.stop, :]
                dv = dv + this * mpost[h : h + 1, :]
                sums[h] = sums[h] + fold(vf * this)
            if c.stop > patches:
                inside = lax.broadcasted_iota(jnp.int32, dv.shape, 0) < patches - c.start
                dv = jnp.where(inside, dv, 0.0)
                vf = jnp.where(inside, vf, 0.0)
            low = dv.astype(BF)
            dqkv_o[i, c, 2 * feats :] = low
            dv_sum = dv_sum + fold(low.astype(F32))
            v_sum = v_sum + fold(vf)
        for h in range(heads):
            acc_o[h : h + 1, :] += colsum(sums[h])
        acc_o[2 * heads : 2 * heads + 1, :] += do_sum * colsum(v_sum)
        acc_o[2 * heads + 10 : 2 * heads + 11, :] += colsum(dv_sum)

        for c in chunks(feats):
            g = c.start // head_dim
            for lane in range(0, slots, 128):
                total = 0.0
                for h in range(heads):
                    total = total + dqs[h, c, lane : lane + 128] * pre_s[h, g]
                dq_t[c, lane : lane + 128] = (total * head_dim**-0.5).astype(BF)
        dq = dq_t[...].T[0:rows]
        dqkv_o[i, :, 0:feats] = dq
        dk_sum = jnp.zeros((8, feats), F32)
        sums = [jnp.zeros((8, feats), F32) for _ in range(heads)]
        for c in chunks(rows):
            kf = k_r[i, c, :].astype(F32)
            dk = 0.0
            for h in range(heads):
                this = dks[h * rows + c.start : h * rows + c.stop, :]
                dk = dk + this * mpre[h : h + 1, :]
                sums[h] = sums[h] + fold(kf * this)
            low = dk.astype(BF)
            dqkv_o[i, c, feats : 2 * feats] = low
            dk_sum = dk_sum + fold(low.astype(F32))
        for h in range(heads):
            acc_o[heads + h : heads + h + 1, :] += colsum(sums[h])
        acc_o[2 * heads + 8 : 2 * heads + 9, :] += colsum(dq.astype(F32))
        acc_o[2 * heads + 9 : 2 * heads + 10, :] += colsum(dk_sum)

        pad[patches:, :] = jnp.zeros((rows - patches, feats), F32)
        pad[0:patches, :] = tok[i].astype(F32)
        da1[...] = nt(dqkv_o[i], wqkv[...])
        gain = row(n1g)
        sums = [jnp.zeros((8, feats), F32) for _ in range(2)]
        for c in chunks(rows):
            n, r = normalized(pad[c, :])
            cot = da1[c, :]
            grad = dx1[i, c, :] + norm_back(cot, n, r, gain)
            sums = [sums[0] + fold(cot * n), sums[1] + fold(cot)]
            if c.stop <= patches:
                in_v[i - first, c, :] = grad
            else:
                in_v[i - first, c.start : patches, :] = grad[0 : patches - c.start]
        for j in range(2):
            acc_o[2 * heads + 11 + j : 2 * heads + 12 + j, :] += colsum(sums[j])
        if first:
            in_copy(i).start()

    if first:
        for i in range(first):
            early_copy(i).wait()

        @pl.loop(first, first + share)
        def _(i):
            in_copy(i).wait()


def qkv_grad_kernel(heads, dqkv, *refs):
    accs = refs[:-8]
    a1, acc_mlp, b1_first, b1_rest, keep, send, small, grads = refs[-8:]
    feats = a1.shape[1]
    count = 2 * keep.shape[0]
    size = 3 * feats // count
    acc = accs[0][...]
    for other in accs[1:]:
        acc = acc + other[...]
    small[...] = jnp.zeros_like(small)
    small[0:2, :] = acc[2 * heads + 11 : 2 * heads + 13]
    small[2:8, :] = acc_mlp[0:6, :]
    small[8:11, :] = acc[2 * heads + 8 : 2 * heads + 11]
    head_dim = feats // heads
    lanes = 2 * heads * heads
    gather = (
        head_of_lane((feats, lanes), 0, head_dim)
        == lax.broadcasted_iota(jnp.int32, (feats, lanes), 1) % heads
    ).astype(F32)
    sums = exact(acc[0 : 2 * heads + 8], gather, ((1,), (0,)))
    place = head_of_lane((2 * heads, lanes), 1, heads) == lax.broadcasted_iota(
        jnp.int32, (2 * heads, lanes), 0
    )
    small[11:12, 0:lanes] = colsum(jnp.where(place, sums[0 : 2 * heads], 0.0))
    small[11:12, lanes : 2 * lanes] = sums[2 * heads : 2 * heads + 1]
    m_idx = lax.axis_index("mp")
    for c, ref in enumerate((b1_first, b1_first, b1_rest, b1_rest)):
        place = 12 + jnp.bitwise_xor(m_idx, c)
        small[pl.ds(place, 1), :] = ref[:, (c % 2) * feats : (c % 2 + 1) * feats]
    low = small[...].astype(BF)
    outs = (keep, send)

    grads[...] = tn(a1[...], dqkv[...]).astype(BF).T

    def put(which, place, b):
        outs[which][place, 0:size, :] = grads[b * size : (b + 1) * size, :]
        outs[which][place, size : size + 16, :] = low
        if outs[which].shape[1] > size + 16:
            outs[which][place, size + 16 :, :] = jnp.zeros_like(outs[which][place, size + 16 :, :])

    store_blocks(count, put)


def final_kernel(heads, size, many, mine, proj_own, *refs):
    got = refs[:many]
    mlp_mine, got_z = refs[many], refs[1 + many : 1 + 2 * many]
    qkv_o, qkvb_o, pre_o, post_o, postb_o, b1_o, *vecs_o, fc1_o, fc2_o, proj_o, held = refs[-18:]
    block, feats = fc1_o.shape
    for place, out in enumerate((fc1_o, fc2_o)):
        rows = slice(place * block, (place + 1) * block)
        out[...] = mlp_mine[rows, :] + sum(g[rows, :].astype(F32) for g in got_z)
    d_idx = lax.axis_index("dp")
    m_idx = lax.axis_index("mp")
    total = mine[...]
    held[m_idx] = proj_own[...].astype(F32)
    for j, part in enumerate(got):
        value = part[...].astype(F32)
        total = total + value[0 : size + 16]
        held[jnp.bitwise_xor(m_idx, j + 1)] = value[size + 16 :]
    proj_o[...] = held[...].reshape(-1, feats)[0:block]
    qkv_o[...] = total[0:size]
    small = total[size : size + 16]

    def own(value, width, index):
        lanes = value.shape[1]
        return pltpu.roll(value, lax.rem(lanes - index * width, lanes), axis=1)[:, 0:width]

    width = vecs_o[0].shape[1]
    vecs = own(small[0:8], width, d_idx)
    for j, ref in enumerate(vecs_o):
        ref[...] = vecs[j : j + 1]
    flat = jnp.concatenate([small[8 + j : 9 + j] for j in range(3)], axis=1)
    qkvb_o[...] = own(jnp.broadcast_to(flat, (8, 3 * feats)), qkvb_o.shape[1], d_idx)[0:1]
    b1 = own(small[8:16], b1_o.shape[1], d_idx)[4:8]
    pick = lax.broadcasted_iota(jnp.int32, b1.shape, 0) == m_idx
    b1_o[...] = colsum(jnp.where(pick, b1, 0.0))
    mix = small[11:12]
    hh = heads * heads
    line = lax.broadcasted_iota(jnp.int32, (heads, hh), 0)
    lane = lax.broadcasted_iota(jnp.int32, (heads, hh), 1)
    fold = (
        lax.broadcasted_iota(jnp.int32, (hh, heads), 0) % heads
        == lax.broadcasted_iota(jnp.int32, (hh, heads), 1)
    ).astype(F32)
    head_dim = feats // heads

    def square(values):
        return exact(jnp.where(lane // heads == line, values, 0.0), fold, ((1,), (0,)))

    post_o[...] = square(mix[:, 0:hh]).T
    pre_o[...] = square(mix[:, hh : 2 * hh]) * (head_dim**-0.5)
    postb_o[...] = mix[:, 2 * hh : 2 * hh + heads]


def whole(shape):
    return pl.BlockSpec(shape, lambda i: (0,) * len(shape))


def each(shape, first=0, many=1):
    return pl.BlockSpec((many,) + shape[1:], lambda i: (i + first,) + (0,) * (len(shape) - 1))


SCALARS = pl.BlockSpec(memory_space=pltpu.SMEM)
IN_VMEM = pl.BlockSpec(memory_space=pltpu.VMEM)
IN_HBM = pl.BlockSpec(memory_space=pltpu.HBM)


def kept(a):
    return pltpu.with_memory_space_constraint(a, pltpu.HBM)


def sds(shape, dtype):
    return jax.ShapeDtypeStruct(shape, dtype)


def call(
    kernel, grid, ins, in_specs, outs, out_specs, scratch=(), flops=0, name=None, aliases=None,
    limit=VMEM_LIMIT,
):
    size = lambda a: a.size * a.dtype.itemsize
    return pl.pallas_call(
        kernel,
        grid=grid,
        in_specs=in_specs,
        out_specs=out_specs,
        out_shape=outs,
        scratch_shapes=scratch,
        input_output_aliases=aliases or {},
        compiler_params=pltpu.CompilerParams(vmem_limit_bytes=limit),
        cost_estimate=pl.CostEstimate(
            flops=flops,
            bytes_accessed=sum(size(a) for a in ins) + sum(size(a) for a in outs),
            transcendentals=0,
        ),
        name=name,
    )(*ins)


def xor_perm(count, mask):
    return [(j, j ^ mask) for j in range(count)]


def dp_hops(dp):
    bits = dp.bit_length() - 1
    groups = []
    at = 1
    while at < bits:
        groups.append((at, min(2, bits - at)))
        at += groups[-1][1]
    return groups


def dp_scatter(value, dp):
    for at, many in dp_hops(dp):
        value = value.reshape((-1, 1 << many) + value.shape[1:])
        got = [
            lax.ppermute(value[:, j].astype(BF), "dp", xor_perm(dp, j << at))
            for j in range(1, 1 << many)
        ]
        value = value[:, 0] + sum(g.astype(F32) for g in got)
    return value.reshape(value.shape[-2:])


def per_device(
    dp, mp,
    tokens_in, image_counts, norm1_gain, norm1_bias, qkv_weight, qkv_bias,
    mix_pre, mix_post, mix_post_bias, proj_weight, proj_bias, gamma1,
    norm2_gain, norm2_bias, fc1_weight, fc1_bias, fc2_weight, fc2_bias, gamma2, out_grad,
):
    images, patches, feats = tokens_in.shape
    heads = mix_pre.shape[0]
    rows = -(-patches // 16) * 16
    slots = -(-patches // 128) * 128
    hidden = fc1_weight.shape[1]
    tok_rows = (images, rows, feats)
    slot_rows = (images, slots, feats)
    prob_shape = (images, heads, rows, slots)
    mix_shape = (heads, feats)
    operands = [
        tokens_in, out_grad, norm1_gain, norm1_bias, qkv_bias, mix_pre, mix_post,
        mix_post_bias, proj_bias, gamma1, norm2_gain, norm2_bias, qkv_weight, proj_weight,
    ]

    ins = [kept(a) for a in [fc1_weight, fc2_weight, fc1_bias] + operands]
    outs = [sds((feats + 16, hidden), BF)] + [sds(a.shape, a.dtype) for a in operands]
    other, *held = call(
        pack_kernel,
        (),
        ins,
        [IN_HBM] * len(ins),
        outs,
        [IN_VMEM] * len(outs),
        [pltpu.VMEM(fc1_bias.shape, F32), pltpu.SemaphoreType.DMA((2 + len(operands),))],
        name="pack",
    )
    near = [lax.ppermute(other, "mp", xor_perm(mp, j)) for j in (1, 2)]

    shares = [images - 1, 1] if images > 1 else [images]
    carried = []
    for s, share in enumerate(shares):
        first = sum(shares[:s])
        ins = [image_counts, mix_post, mix_post_bias] + held
        outs = call(
            functools.partial(attn_fwd_kernel, first, share),
            (),
            ins + carried,
            [SCALARS] * 3
            + [IN_VMEM] * 14
            + [pl.BlockSpec(memory_space=pl.ANY)] * len(carried),
            [
                sds(tok_rows, BF), sds(slot_rows, BF), sds(tok_rows, BF), sds(tok_rows, BF),
                sds(prob_shape, BF), sds(tok_rows, BF), sds(tok_rows, F32), sds(tok_rows, F32),
                sds(tok_rows, BF), sds(tok_rows, BF), sds(mix_shape, F32), sds(mix_shape, F32),
                sds((1, feats), F32),
            ],
            [IN_VMEM] * 13,
            [
                pltpu.VMEM((rows, feats), F32), pltpu.VMEM((heads * rows, 2 * feats), BF),
                pltpu.VMEM((feats, slots), BF), pltpu.VMEM((rows, 3 * feats), F32), pltpu.VMEM((heads * rows, slots), F32),
                pltpu.VMEM((heads, feats, slots), F32),
            ],
            flops=share * 15 * 10**8,
            name="attn_fwd",
            aliases={len(ins) + j: j for j in range(10)} if carried else None,
        )
        carried, (mpre, mpost, mixb) = list(outs[:10]), outs[10:]
        if s == 0:
            near, carried[0] = lax.optimization_barrier((near, carried[0]))
            last = lax.ppermute(near[1], "mp", xor_perm(mp, 1))
            near = jnp.stack(near)
            far = lax.ppermute(near, "dp", xor_perm(dp, 1))
    a1, q, k, v, prob, o, x1, u, a2, dy = carried
    far, a2 = lax.optimization_barrier((far, a2))

    block = feats // dp
    total = images * rows
    flat = (total, feats)
    a2, dy, x1, u, o = (a.reshape(flat) for a in (a2, dy, x1, u, o))
    ins = [a2, dy, gamma2, fc1_weight, fc1_bias, fc2_weight, near, far]
    wide = 2 * hidden
    grad_shape = (2, wide, feats)
    f0, da20, hids, dzs, dfs = call(
        mlp_first_kernel,
        (),
        ins,
        [IN_VMEM] * len(ins),
        [
            sds(flat, F32), sds(flat, F32), sds((total, wide), BF), sds((total, wide), BF),
            sds(flat, BF),
        ],
        [IN_VMEM] * 5,
        [
            pltpu.VMEM((feats, wide), BF), pltpu.VMEM((wide, feats), BF),
            pltpu.VMEM((1, wide), F32),
            pltpu.VMEM((2, total // 3, 256), F32), pltpu.VMEM((2, total // 3, 256), F32),
        ],
        flops=images * 5 * 10**8,
        name="mlp_first",
    )

    last, f0 = lax.optimization_barrier((last, f0))
    far_last = lax.ppermute(last, "dp", xor_perm(dp, 1))
    ins = [a2, hids, dzs, dfs]
    grads0, b1_0, a2t, dft = call(
        mlp_grad_kernel,
        (),
        ins,
        [IN_VMEM] * 4,
        [
            sds(grad_shape, BF), sds((1, wide), F32), sds((feats + 16, total), BF),
            sds((feats, total), BF),
        ],
        [IN_VMEM] * 4,
        flops=images * 3 * 10**8,
        name="mlp_grad",
    )

    grad_rows = 9 * block
    half_shape = (dp // 2, grad_rows, feats)
    ins = [
        image_counts, a2, dy, dfs, x1, u, o, f0, da20, near, far, last, far_last, grads0, a2t, dft,
        proj_weight, gamma1,
        norm2_gain, fc2_bias, gamma2,
    ]
    layer_out, dx1, do, keep, send, b1_1, acc_mlp = call(
        mlp_rest_kernel,
        (),
        ins,
        [SCALARS] + [IN_VMEM] * (len(ins) - 1),
        [
            sds(tokens_in.shape, BF), sds(flat, F32), sds(slot_rows, BF), sds(half_shape, BF),
            sds(half_shape, BF), sds((1, wide), F32), sds((8, feats), F32),
        ],
        [IN_HBM] + [IN_VMEM] * 6,
        [
            pltpu.VMEM((feats, wide), BF), pltpu.VMEM((wide, feats), BF),
            pltpu.VMEM((1, wide), F32), pltpu.VMEM((total, wide), BF),
            pltpu.VMEM((total, wide), BF),
            pltpu.VMEM((2, total // 3, 256), F32), pltpu.VMEM((2, total // 3, 256), F32),
            pltpu.VMEM(flat, F32), pltpu.VMEM(flat, F32), pltpu.VMEM(flat, BF),
            pltpu.VMEM((wide, feats), BF), pltpu.VMEM((feats, wide), BF),
            pltpu.VMEM((feats, feats), BF), pltpu.VMEM(tokens_in.shape, BF),
            pltpu.SemaphoreType.DMA((images,)),
        ],
        flops=images * 9 * 10**8,
        name="mlp_rest",
    )
    got = lax.ppermute(send, "dp", xor_perm(dp, 1))
    dx1 = dx1.reshape(tok_rows)

    shares = [1, images - 1] if images > 1 else [1]
    dqkv_shape = (images, rows, 3 * feats)
    carried, accs = [], []
    for s, share in enumerate(shares):
        first = sum(shares[:s])
        ins = [mix_pre, do, q, k, v, prob, dx1, tokens_in, mpre, mpost, mixb, qkv_weight, norm1_gain]
        in_shape = tokens_in.shape if first or share == images else (share,) + tokens_in.shape[1:]
        *carried, acc = call(
            functools.partial(attn_bwd_kernel, first, share),
            (),
            ins + carried,
            [SCALARS]
            + [IN_VMEM] * (len(ins) - 1)
            + [pl.BlockSpec(memory_space=pl.ANY), IN_VMEM][: len(carried)],
            [sds(dqkv_shape, BF), sds(in_shape, F32), sds((2 * heads + 16, feats), F32)],
            [IN_VMEM, IN_HBM if first else IN_VMEM, IN_VMEM],
            [
                pltpu.VMEM((heads * rows, feats), BF), pltpu.VMEM((heads * rows, slots), BF),
                pltpu.VMEM((feats, slots), BF), pltpu.VMEM((heads * rows, slots), F32),
                pltpu.VMEM((heads * rows, feats), F32), pltpu.VMEM((heads * rows, feats), F32),
                pltpu.VMEM((heads, feats, slots), F32), pltpu.VMEM((rows, feats), F32),
                pltpu.VMEM((rows, feats), F32),
            ]
            + [pltpu.VMEM((share, patches, feats), F32), pltpu.SemaphoreType.DMA((images,))]
            * bool(first),
            flops=share * 20 * 10**8,
            name="attn_bwd",
            aliases={len(ins): 0} if carried else None,
        )
        accs.append(acc)
        if s == 0:
            (keep, got), acc = lax.optimization_barrier(((keep, got), acc))
            mine = dp_scatter(keep.astype(F32) + got.astype(F32), dp)
            accs[0], do = lax.optimization_barrier((acc, do))
    dqkv, in_grad = carried
    mine, dqkv = lax.optimization_barrier((mine, dqkv))
    mlp_mine = mine
    low = mine.astype(BF)
    m_idx = lax.axis_index("mp")
    share_rows = -(-block // (16 * mp)) * 16
    proj = jnp.pad(mine[8 * block :], ((0, mp * share_rows - block), (0, 0)))

    def proj_share(j):
        return lax.dynamic_slice_in_dim(proj, jnp.bitwise_xor(m_idx, j) * share_rows, share_rows)

    got_z = [
        lax.ppermute(
            jnp.concatenate([low[2 * j * block : 2 * (j + 1) * block], proj_share(j).astype(BF)]),
            "mp",
            xor_perm(mp, j),
        )
        for j in range(1, mp)
    ]

    q_block = 3 * feats // dp
    half_shape = (dp // 2, q_block + 16, feats)
    ins = [dqkv.reshape(total, 3 * feats)] + accs + [a1.reshape(flat), acc_mlp, b1_0, b1_1]
    keep, send = call(
        functools.partial(qkv_grad_kernel, heads),
        (),
        ins,
        [IN_VMEM] * len(ins),
        [sds(half_shape, BF), sds(half_shape, BF)],
        [IN_VMEM] * 2,
        [pltpu.VMEM((16, feats), F32), pltpu.VMEM((3 * feats, feats), BF)],
        flops=11 * 10**8,
        name="qkv_grad",
    )
    got = lax.ppermute(send, "dp", xor_perm(dp, 1))
    mine = dp_scatter(keep.astype(F32) + got.astype(F32), dp)
    mine, got_z = lax.optimization_barrier((mine, got_z))

    proj_own = (proj_share(0) + sum(g[2 * block :].astype(F32) for g in got_z)).astype(BF)
    payload = jnp.concatenate([mine.astype(BF), proj_own])
    got = [lax.ppermute(payload, "mp", xor_perm(mp, j)) for j in range(1, mp)]
    b1_size = hidden // dp
    ins = [mine, proj_own] + got + [mlp_mine] + got_z
    outs = [
        sds((q_block, feats), F32), sds((1, q_block), F32), sds((heads, heads), F32),
        sds((heads, heads), F32), sds((1, heads), F32), sds((1, b1_size), F32),
    ] + [sds((1, block), F32)] * 8 + [sds((block, feats), F32)] * 3
    qkvw, qkvb, pre, post, postb, b1g, *vecs, fc1g, fc2g, projg = call(
        functools.partial(final_kernel, heads, q_block, mp - 1),
        (),
        ins,
        [IN_VMEM] * len(ins),
        outs,
        [IN_VMEM] * len(outs),
        [pltpu.VMEM((mp, share_rows, feats), F32)],
        name="final",
    )
    vecs = [a.reshape(-1) for a in vecs]
    return (
        layer_out,
        in_grad,
        vecs[0],
        vecs[1],
        qkvw.T,
        qkvb.reshape(-1),
        pre,
        post,
        postb.reshape(-1),
        projg.T,
        vecs[2],
        vecs[3],
        vecs[4],
        vecs[5],
        fc1g.T,
        b1g.reshape(-1),
        fc2g.T,
        vecs[6],
        vecs[7],
    )


def solution(mesh):
    tokens = P(("dp", "mp"), None, None)
    placed = (
        (tokens, P("dp")) + (P(),) * 12 + (P(None, "mp"), P("mp"), P("mp", None), P(), P(), tokens)
    )
    return jax.shard_map(
        functools.partial(per_device, mesh.shape["dp"], mesh.shape["mp"]),
        mesh=mesh,
        in_specs=placed,
        out_specs=(
            tokens, tokens, P("dp"), P("dp"), P(None, "dp"), P("dp"), P(), P(), P(),
            P(None, "dp"), P("dp"), P("dp"), P("dp"), P("dp"), P(None, ("mp", "dp")),
            P(("mp", "dp")), P("mp", "dp"), P("dp"), P("dp"),
        ),
        check_vma=False,
    )
```

profile of v0, /device:TPU:0, one launch (start us, length us, event | category | flops | bytes accessed | tf_op | source)
XLA Modules:
  0.0 99.8 jit_solution(12496232469791157527)
XLA Ops:
  0.7 0.0 copy-start.5
  0.7 0.0 copy-start.11
  0.7 2.2 %pack.1 = (bf16[400,384]{1,0:T(8,128)(2,1)S(1)}, bf16[6,196,384]{2,1,0:T(8,128)(2,1)S(1)}, bf16[6,196,384]{2,1,0:T(8,128)(2,1)S(1)}, f32[384]{0:T(512)S(1)}, f32...) custom-call(bf16[384,384]{1,0:T(8,128)(2,1)} %w1_own.1, ...), custom_call_target="tpu_custom_call" | custom-call | bytes 6899264 | tf_op jit(solution)/shard_map/pack/pallas_call | solution.py:658
  2.9 3.1 %collective-permute-start = (bf16[400,384]{1,0:T(8,128)(2,1)S(1)}, bf16[400,384]{1,0:T(8,128)(2,1)S(1)}, u32[]{:S(2)}, u32[]{:S(2)}) collective-permute-start(bf16[400,384]{1,0:T(8,128)(2,1)S(1)} %get-tuple-element.116), channel_id=1, source_target_pairs={{0,1},{1,0},{2,3},{3,2},{4,5},{5,4},{6,7},{7,6},{8,9},{9,8},{10,11... | collective-permute-start | bytes 921608 | tf_op jit(solution)/shard_map/ppermute | solution.py:733
  6.0 2.6 %collective-permute-start.1 = (bf16[400,384]{1,0:T(8,128)(2,1)S(1)}, bf16[400,384]{1,0:T(8,128)(2,1)S(1)}, u32[]{:S(2)}, u32[]{:S(2)}) collective-permute-start(bf16[400,384]{1,0:T(8,128)(2,1)S(1)} %get-tuple-element.116), channel_id=1, source_target_pairs={{0,2},{1,3},{2,0},{3,1},{4,6},{5,7},{6,4},{7,5},{8,10},{9,11},{10,... | collective-permute-start | bytes 921608 | tf_op jit(solution)/shard_map/ppermute | solution.py:733
  9.2 0.0 copy-done.5
  9.2 0.0 copy-done.11
  9.2 14.8 %attn_fwd.2 = (bf16[6,208,384]{2,1,0:T(8,128)(2,1)S(1)}, bf16[6,256,384]{2,1,0:T(8,128)(2,1)S(1)}, bf16[6,208,384]{2,1,0:T(8,128)(2,1)S(1)}, bf16[6,208,384]{2,1...) custom-call(s32[1]{0:T(128)S(6)} %copy.61.refs_0_.counts, ...), custom_call_target="tpu_custom_call" | custom-call | flops 7500000256 | bytes 18902852 | tf_op jit(solution)/shard_map/attn_fwd/pallas_call | solution.py:658
  24.0 0.0 collective-permute-done
  24.0 0.0 collective-permute-done.1
  24.0 0.1 pad_maximum_fusion.near
  24.1 0.1 collective-permute-start.2
  24.2 0.5 collective-permute-start.3
  24.7 3.5 %attn_fwd.3 = (bf16[6,208,384]{2,1,0:T(8,128)(2,1)S(1)}, bf16[6,256,384]{2,1,0:T(8,128)(2,1)S(1)}, bf16[6,208,384]{2,1,0:T(8,128)(2,1)S(1)}, bf16[6,208,384]{2,1...) custom-call(s32[1]{0:T(128)S(6)} %copy.61.refs_0_.counts, ...), custom_call_target="tpu_custom_call", output_to_operand_aliasing={{0}: (17, {}), {1}: (18, {}), {2}: (19, {}), {3}: (20, {}),... | custom-call | flops 1500000000 | bytes 34778948 | tf_op jit(solution)/shard_map/attn_fwd/pallas_call | solution.py:658
  28.2 0.0 collective-permute-done.2.far
  28.2 0.0 copy-done.2
  28.2 6.2 %mlp_first.1 = (f32[1248,384]{1,0:T(8,128)S(1)}, f32[1248,384]{1,0:T(8,128)S(1)}, bf16[1248,768]{1,0:T(8,128)(2,1)S(1)}, bf16[1248,768]{1,0:T(8,128)(2,1)S(1)}, bf16[1248,384]{1,0:T(8,128)(2,1)S(1)}) custom-call(bf16[1248,384]{1,0:T(8,128)(2,1)S(1)} %bitcast.67, bf16[1248,384]{1,0:T(8,128)(2,1)S(1)} %bitcast.70, f32[384]{0:T(512)S(1)} %copy-done.12, ...), custom_call_target="tpu_custom_call" | custom-call | flops 3000000000 | bytes 12364800 | tf_op jit(solution)/shard_map/mlp_first/pallas_call | solution.py:658
  34.4 0.0 collective-permute-done.3.last
  34.4 0.2 collective-permute-start.4
  34.7 1.8 %mlp_grad.1 = (bf16[2,768,384]{2,1,0:T(8,128)(2,1)S(1)}, f32[1,768]{1,0:T(1,128)S(1)}, bf16[400,1248]{1,0:T(8,128)(2,1)S(1)}, bf16[384,1248]{1,0:T(8,128)(2,1)S(1)}) custom-call(bf16[1248,384]{1,0:T(8,128)(2,1)S(1)} %bitcast.68, bf16[1248,768]{1,0:T(8,128)(2,1)S(1)} %get-tuple-element.156.hids, bf16[1248,768]{1,0:T(8,128)(2,1)S(1)} %get-tuple-element.157.dzs, ...), custom_call_target="tpu_custom_call" | custom-call | flops 1800000000 | bytes 8890368 | tf_op jit(solution)/shard_map/mlp_grad/pallas_call | solution.py:658
  36.5 0.0 collective-permute-done.4.far_last
  36.5 0.0 copy-start
  36.6 0.0 copy-start.1
  36.6 0.0 copy-start.6
  36.6 0.0 copy-start.7
  36.6 11.3 %mlp_rest.1 = (bf16[6,196,384]{2,1,0:T(8,128)(2,1)}, f32[1248,384]{1,0:T(8,128)S(1)}, bf16[6,256,384]{2,1,0:T(8,128)(2,1)S(1)}, bf16[4,432,384]{2,1,0:T(8,128)(2...) custom-call(s32[1]{0:T(128)S(6)} %copy.61.refs_0_.counts, ...), custom_call_target="tpu_custom_call" | custom-call | flops 5400000000 | bytes 23451652 | tf_op jit(solution)/shard_map/mlp_rest/pallas_call | solution.py:658
  47.9 0.4 collective-permute-start.5
  48.4 0.0 copy-done.1
  48.4 3.4 %attn_bwd.2 = (bf16[6,208,1152]{2,1,0:T(8,128)(2,1)S(1)}, f32[1,196,384]{2,1,0:T(8,128)S(1)}, f32[32,384]{1,0:T(8,128)S(1)}) custom-call(f32[8,8]{1,0:T(8,128)S(1)} %copy-done.6, bf16[6,256,384]{2,1,0:T(8,128)(2,1)S(1)} %get-tuple-element.175.refs_1_, bf16[6,256,384]{2,1,0:T(8,128)(2,1)S(1)} %get-tuple-element.165.refs_2_, ...), custom_call_target="tpu_custom_call" | custom-call | flops 2000000000 | bytes 16346368 | tf_op jit(solution)/shard_map/attn_bwd/pallas_call | solution.py:658
  51.8 0.0 collective-permute-done.5
  51.8 0.4 fusion.10
  52.2 0.1 slice_bitcast_fusion.3
  52.3 1.6 %collective-permute-start.6 = (bf16[1,432,384]{2,1,0:T(8,128)(2,1)S(1)}, bf16[1,432,384]{2,1,0:T(8,128)(2,1)S(1)}, u32[]{:S(2)}, u32[]{:S(2)}) collective-permute-start(bf16[1,432,384]{2,1,0:T(8,128)(2,1)S(1)} %get-tuple-element.215), channel_id=1, source_target_pairs={{0,8},{4,12},{8,0},{12,4},{16,24},{20,28},{24,16},{28,20},{1,9},{5... | collective-permute-start | bytes 995336 | tf_op jit(solution)/shard_map/ppermute | solution.py:694
  53.8 1.5 %collective-permute-start.7 = (bf16[1,432,384]{2,1,0:T(8,128)(2,1)S(1)}, bf16[1,432,384]{2,1,0:T(8,128)(2,1)S(1)}, u32[]{:S(2)}, u32[]{:S(2)}) collective-permute-start(bf16[1,432,384]{2,1,0:T(8,128)(2,1)S(1)} %get-tuple-element.217), channel_id=1, source_target_pairs={{0,16},{4,20},{8,24},{12,28},{16,0},{20,4},{24,8},{28,12},{1,17},{... | collective-permute-start | bytes 995336 | tf_op jit(solution)/shard_map/ppermute | solution.py:694
  55.3 0.5 collective-permute-start.8
  55.8 15.1 %attn_bwd.3 = (bf16[6,208,1152]{2,1,0:T(8,128)(2,1)S(1)}, f32[6,196,384]{2,1,0:T(8,128)}, f32[32,384]{1,0:T(8,128)S(1)}) custom-call(f32[8,8]{1,0:T(8,128)S(1)} %copy-done.6, bf16[6,256,384]{2,1,0:T(8,128)(2,1)S(1)} %get-tuple-element.175.refs_1_, bf16[6,256,384]{2,1,0:T(8,128)(2,1)S(1)} %get-tuple-element.165.refs_2_, ...), custom_call_target="tpu_custom_call", output_to_operand_aliasing={{0}: (13, {})} | custom-call | flops 10000000000 | bytes 21028096 | tf_op jit(solution)/shard_map/attn_bwd/pallas_call | solution.py:658
  70.9 0.0 collective-permute-done.6
  70.9 0.0 collective-permute-done.7
  70.9 0.0 collective-permute-done.8
  70.9 0.1 fusion.1.refs_3_
  71.1 1.7 %qkv_grad.1 = (bf16[4,160,384]{2,1,0:T(8,128)(2,1)S(1)}, bf16[4,160,384]{2,1,0:T(8,128)(2,1)S(1)}) custom-call(bf16[1248,1152]{1,0:T(8,128)(2,1)S(1)} %bitcast.72, f32[32,384]{1,0:T(8,128)S(1)} %get-tuple-element.183.refs_0_, f32[32,384]{1,0:T(8,128)S(1)} %get-tuple-element.184.refs_1_, bf16[1248,384]{1,0:T(8,128)(2,1)S(1)} %bitcast.65, ...), custom_call_target="tpu_custom_call" | custom-call | flops 1100000000 | bytes 4933632 | tf_op jit(solution)/shard_map/qkv_grad/pallas_call | solution.py:658
  72.8 0.1 collective-permute-start.9
  73.1 1.4 %collective-permute-start.15 = (bf16[112,384]{1,0:T(8,128)(2,1)S(1)}, bf16[112,384]{1,0:T(8,128)(2,1)S(1)}, u32[]{:S(2)}, u32[]{:S(2)}) collective-permute-start(bf16[112,384]{1,0:T(8,128)(2,1)S(1)} %pad_maximum_fusion.4), channel_id=1, source_target_pairs={{0,3},{1,2},{2,1},{3,0},{4,7},{5,6},{6,5},{7,4},{8,11},{9,10},{10,... | collective-permute-start | bytes 258056 | tf_op jit(solution)/shard_map/ppermute | solution.py:894
  74.5 0.3 collective-permute-done.9
  74.8 0.1 fusion.9
  74.9 1.6 %collective-permute-start.10 = (bf16[1,160,384]{2,1,0:T(8,128)(2,1)S(1)}, bf16[1,160,384]{2,1,0:T(8,128)(2,1)S(1)}, u32[]{:S(2)}, u32[]{:S(2)}) collective-permute-start(bf16[1,160,384]{2,1,0:T(8,128)(2,1)S(1)} %get-tuple-element.220), channel_id=1, source_target_pairs={{0,8},{4,12},{8,0},{12,4},{16,24},{20,28},{24,16},{28,20},{1,9},{5... | collective-permute-start | bytes 368648 | tf_op jit(solution)/shard_map/ppermute | solution.py:694
  76.5 1.5 %collective-permute-start.11 = (bf16[1,160,384]{2,1,0:T(8,128)(2,1)S(1)}, bf16[1,160,384]{2,1,0:T(8,128)(2,1)S(1)}, u32[]{:S(2)}, u32[]{:S(2)}) collective-permute-start(bf16[1,160,384]{2,1,0:T(8,128)(2,1)S(1)} %get-tuple-element.222), channel_id=1, source_target_pairs={{0,16},{4,20},{8,24},{12,28},{16,0},{20,4},{24,8},{28,12},{1,17},{... | collective-permute-start | bytes 368648 | tf_op jit(solution)/shard_map/ppermute | solution.py:694
  78.0 0.5 collective-permute-start.12
  78.5 1.5 %collective-permute-start.14 = (bf16[112,384]{1,0:T(8,128)(2,1)S(1)}, bf16[112,384]{1,0:T(8,128)(2,1)S(1)}, u32[]{:S(2)}, u32[]{:S(2)}) collective-permute-start(bf16[112,384]{1,0:T(8,128)(2,1)S(1)} %pad_maximum_fusion.3), channel_id=1, source_target_pairs={{0,2},{1,3},{2,0},{3,1},{4,6},{5,7},{6,4},{7,5},{8,10},{9,11},{10,... | collective-permute-start | bytes 258056 | tf_op jit(solution)/shard_map/ppermute | solution.py:894
  80.0 0.5 collective-permute-done.10
  80.5 1.6 %collective-permute-start.13 = (bf16[112,384]{1,0:T(8,128)(2,1)S(1)}, bf16[112,384]{1,0:T(8,128)(2,1)S(1)}, u32[]{:S(2)}, u32[]{:S(2)}) collective-permute-start(bf16[112,384]{1,0:T(8,128)(2,1)S(1)} %pad_maximum_fusion.2), channel_id=1, source_target_pairs={{0,1},{1,0},{2,3},{3,2},{4,5},{5,4},{6,7},{7,6},{8,9},{9,8},{10,11... | collective-permute-start | bytes 258056 | tf_op jit(solution)/shard_map/ppermute | solution.py:894
  82.1 2.1 %collective-permute-done.11 = bf16[1,160,384]{2,1,0:T(8,128)(2,1)S(1)} collective-permute-done((bf16[1,160,384]{2,1,0:T(8,128)(2,1)S(1)}, bf16[1,160,384]{2,1,0:T(8,128)(2,1)S(1)}, u32[]{:S(2)}, u32[]{:S(2)}) %collective-permute-start.11) | collective-permute-done | bytes 122912 | tf_op jit(solution)/shard_map/ppermute | solution.py:694
  84.2 0.0 collective-permute-done.12
  84.2 0.1 fusion.3.mine
  84.3 0.0 collective-permute-done.15.refs_6_
  84.3 0.0 collective-permute-done.14.refs_5_
  84.3 0.8 collective-permute-done.13.refs_4_
  85.2 1.5 %collective-permute-start.16 = (bf16[176,384]{1,0:T(8,128)(2,1)S(1)}, bf16[176,384]{1,0:T(8,128)(2,1)S(1)}, u32[]{:S(2)}, u32[]{:S(2)}) collective-permute-start(bf16[176,384]{1,0:T(8,128)(2,1)S(1)} %pad_maximum_fusion.1), channel_id=1, source_target_pairs={{0,1},{1,0},{2,3},{3,2},{4,5},{5,4},{6,7},{7,6},{8,9},{9,8},{10,11... | collective-permute-start | bytes 405512 | tf_op jit(solution)/shard_map/ppermute | solution.py:922
  86.7 2.0 %collective-permute-start.17 = (bf16[176,384]{1,0:T(8,128)(2,1)S(1)}, bf16[176,384]{1,0:T(8,128)(2,1)S(1)}, u32[]{:S(2)}, u32[]{:S(2)}) collective-permute-start(bf16[176,384]{1,0:T(8,128)(2,1)S(1)} %pad_maximum_fusion.1), channel_id=1, source_target_pairs={{0,2},{1,3},{2,0},{3,1},{4,6},{5,7},{6,4},{7,5},{8,10},{9,11},{10,... | collective-permute-start | bytes 405512 | tf_op jit(solution)/shard_map/ppermute | solution.py:922
  88.7 0.9 collective-permute-start.18
  89.6 1.7 %collective-permute-done.16.refs_0_ = bf16[176,384]{1,0:T(8,128)(2,1)S(1)} collective-permute-done((bf16[176,384]{1,0:T(8,128)(2,1)S(1)}, bf16[176,384]{1,0:T(8,128)(2,1)S(1)}, u32[]{:S(2)}, u32[]{:S(2)}) %collective-permute-start.16) | collective-permute-done | bytes 135200 | tf_op jit(solution)/shard_map/ppermute | solution.py:922
  91.4 7.2 %collective-permute-done.17.refs_1_ = bf16[176,384]{1,0:T(8,128)(2,1)S(1)} collective-permute-done((bf16[176,384]{1,0:T(8,128)(2,1)S(1)}, bf16[176,384]{1,0:T(8,128)(2,1)S(1)}, u32[]{:S(2)}, u32[]{:S(2)}) %collective-permute-start.17) | collective-permute-done | bytes 135200 | tf_op jit(solution)/shard_map/ppermute | solution.py:922
  98.6 0.0 collective-permute-done.18.refs_2_
  98.6 1.0 final.1
  (29 shorter events, 0.3 us)
Async XLA Ops:
  0.7 8.5 %copy-start.5 = (f32[8,8]{1,0:T(8,128)S(1)}, f32[8,8]{1,0:T(8,128)}, u32[]{:S(2)}) copy-start(f32[8,8]{1,0:T(8,128)} %refs_1_.5) | copy-start | bytes 772
  0.7 8.5 %copy-start.11 = (f32[8]{0:T(128)S(1)}, f32[8]{0:T(128)}, u32[]{:S(2)}) copy-start(f32[8]{0:T(128)} %refs_2_.5) | copy-start | bytes 100
  2.9 21.2 %collective-permute-start = (bf16[400,384]{1,0:T(8,128)(2,1)S(1)}, bf16[400,384]{1,0:T(8,128)(2,1)S(1)}, u32[]{:S(2)}, u32[]{:S(2)}) collective-permute-start(bf16[400,384]{1,0:T(8,128)(2,1)S(1)} %get-tuple-element.116), channel_id=1, source_target_pairs={{0,1},{1,0},{2,3},{3,2},{4,5},{5,4},{6,7},{7,6},{8,9},{9,8},{10,11... | collective-permute-start | bytes 921608 | tf_op jit(solution)/shard_map/ppermute | solution.py:733
  6.0 18.1 %collective-permute-start.1 = (bf16[400,384]{1,0:T(8,128)(2,1)S(1)}, bf16[400,384]{1,0:T(8,128)(2,1)S(1)}, u32[]{:S(2)}, u32[]{:S(2)}) collective-permute-start(bf16[400,384]{1,0:T(8,128)(2,1)S(1)} %get-tuple-element.116), channel_id=1, source_target_pairs={{0,2},{1,3},{2,0},{3,1},{4,6},{5,7},{6,4},{7,5},{8,10},{9,11},{10,... | collective-permute-start | bytes 921608 | tf_op jit(solution)/shard_map/ppermute | solution.py:733
  24.1 4.1 %collective-permute-start.2 = (bf16[2,400,384]{2,1,0:T(8,128)(2,1)S(1)}, bf16[2,400,384]{2,1,0:T(8,128)(2,1)S(1)}, u32[]{:S(2)}, u32[]{:S(2)}) collective-permute-start(bf16[2,400,384]{2,1,0:T(8,128)(2,1)S(1)} %pad_maximum_fusion.near), channel_id=1, source_target_pairs={{0,4},{4,0},{8,12},{12,8},{16,20},{20,16},{24,28},{28,24},{1,5},{5... | collective-permute-start | bytes 1843208 | tf_op jit(solution)/shard_map/ppermute | solution.py:768
  24.2 10.3 %collective-permute-start.3 = (bf16[400,384]{1,0:T(8,128)(2,1)S(1)}, bf16[400,384]{1,0:T(8,128)(2,1)S(1)}, u32[]{:S(2)}, u32[]{:S(2)}) collective-permute-start(bf16[400,384]{1,0:T(8,128)(2,1)S(1)} %collective-permute-done.1), channel_id=1, source_target_pairs={{0,1},{1,0},{2,3},{3,2},{4,5},{5,4},{6,7},{7,6},{8,9},{9,8},{10,11... | collective-permute-start | bytes 921608 | tf_op jit(solution)/shard_map/ppermute | solution.py:766
  24.7 3.5 %copy-start.2 = (bf16[384,384]{1,0:T(8,128)(2,1)S(1)}, bf16[384,384]{1,0:T(8,128)(2,1)}, u32[]{:S(2)}) copy-start(bf16[384,384]{1,0:T(8,128)(2,1)} %w1_own.1) | copy-start | bytes 884740
  24.7 3.5 %copy-start.3 = (bf16[384,384]{1,0:T(8,128)(2,1)S(1)}, bf16[384,384]{1,0:T(8,128)(2,1)}, u32[]{:S(2)}) copy-start(bf16[384,384]{1,0:T(8,128)(2,1)} %w2_own.1) | copy-start | bytes 884740
  24.7 3.5 %copy-start.8 = (f32[384]{0:T(512)S(1)}, f32[384]{0:T(512)}, u32[]{:S(2)}) copy-start(f32[384]{0:T(512)} %b1_own.1) | copy-start | bytes 4612
  24.7 3.5 %copy-start.12 = (f32[384]{0:T(512)S(1)}, f32[384]{0:T(512)}, u32[]{:S(2)}) copy-start(f32[384]{0:T(512)} %gamma2.3) | copy-start | bytes 4612
  34.4 2.0 %collective-permute-start.4 = (bf16[400,384]{1,0:T(8,128)(2,1)S(1)}, bf16[400,384]{1,0:T(8,128)(2,1)S(1)}, u32[]{:S(2)}, u32[]{:S(2)}) collective-permute-start(bf16[400,384]{1,0:T(8,128)(2,1)S(1)} %collective-permute-done.3.last), channel_id=1, source_target_pairs={{0,4},{4,0},{8,12},{12,8},{16,20},{20,16},{24,28},{28,24},{1,5},{5... | collective-permute-start | bytes 921608 | tf_op jit(solution)/shard_map/ppermute | solution.py:799
  34.7 1.8 %copy-start.4 = (bf16[384,384]{1,0:T(8,128)(2,1)S(1)}, bf16[384,384]{1,0:T(8,128)(2,1)}, u32[]{:S(2)}) copy-start(bf16[384,384]{1,0:T(8,128)(2,1)} %wproj.1) | copy-start | bytes 884740
  34.7 1.8 %copy-start.9 = (f32[384]{0:T(512)S(1)}, f32[384]{0:T(512)}, u32[]{:S(2)}) copy-start(f32[384]{0:T(512)} %gamma1.1) | copy-start | bytes 4612
  34.7 1.8 %copy-start.10 = (f32[384]{0:T(512)S(1)}, f32[384]{0:T(512)}, u32[]{:S(2)}) copy-start(f32[384]{0:T(512)} %n2g.1) | copy-start | bytes 4612
  34.7 1.8 %copy-start.13 = (f32[384]{0:T(512)S(1)}, f32[384]{0:T(512)}, u32[]{:S(2)}) copy-start(f32[384]{0:T(512)} %fc2b.1) | copy-start | bytes 4612
  36.5 11.8 %copy-start = (bf16[6,196,384]{2,1,0:T(8,128)(2,1)S(1)}, bf16[6,196,384]{2,1,0:T(8,128)(2,1)}, u32[]{:S(2)}) copy-start(bf16[6,196,384]{2,1,0:T(8,128)(2,1)} %refs_7_.5) | copy-start | bytes 2709508
  36.6 11.8 %copy-start.1 = (bf16[384,1152]{1,0:T(8,128)(2,1)S(1)}, bf16[384,1152]{1,0:T(8,128)(2,1)}, u32[]{:S(2)}) copy-start(bf16[384,1152]{1,0:T(8,128)(2,1)} %refs_11_.5) | copy-start | bytes 2654212
  36.6 11.8 %copy-start.6 = (f32[8,8]{1,0:T(8,128)S(1)}, f32[8,8]{1,0:T(8,128)}, u32[]{:S(2)}) copy-start(f32[8,8]{1,0:T(8,128)} %refs_0_.7) | copy-start | bytes 772
  36.6 11.8 %copy-start.7 = (f32[384]{0:T(512)S(1)}, f32[384]{0:T(512)}, u32[]{:S(2)}) copy-start(f32[384]{0:T(512)} %refs_12_.5) | copy-start | bytes 4612
  47.9 3.9 %collective-permute-start.5 = (bf16[4,432,384]{2,1,0:T(8,128)(2,1)S(1)}, bf16[4,432,384]{2,1,0:T(8,128)(2,1)S(1)}, u32[]{:S(2)}, u32[]{:S(2)}) collective-permute-start(bf16[4,432,384]{2,1,0:T(8,128)(2,1)S(1)} %get-tuple-element.163), channel_id=1, source_target_pairs={{0,4},{4,0},{8,12},{12,8},{16,20},{20,16},{24,28},{28,24},{1,5},{5... | collective-permute-start | bytes 3981320 | tf_op jit(solution)/shard_map/ppermute | solution.py:845
  52.3 18.6 %collective-permute-start.6 = (bf16[1,432,384]{2,1,0:T(8,128)(2,1)S(1)}, bf16[1,432,384]{2,1,0:T(8,128)(2,1)S(1)}, u32[]{:S(2)}, u32[]{:S(2)}) collective-permute-start(bf16[1,432,384]{2,1,0:T(8,128)(2,1)S(1)} %get-tuple-element.215), channel_id=1, source_target_pairs={{0,8},{4,12},{8,0},{12,4},{16,24},{20,28},{24,16},{28,20},{1,9},{5... | collective-permute-start | bytes 995336 | tf_op jit(solution)/shard_map/ppermute | solution.py:694
  53.8 17.1 %collective-permute-start.7 = (bf16[1,432,384]{2,1,0:T(8,128)(2,1)S(1)}, bf16[1,432,384]{2,1,0:T(8,128)(2,1)S(1)}, u32[]{:S(2)}, u32[]{:S(2)}) collective-permute-start(bf16[1,432,384]{2,1,0:T(8,128)(2,1)S(1)} %get-tuple-element.217), channel_id=1, source_target_pairs={{0,16},{4,20},{8,24},{12,28},{16,0},{20,4},{24,8},{28,12},{1,17},{... | collective-permute-start | bytes 995336 | tf_op jit(solution)/shard_map/ppermute | solution.py:694
  55.3 15.6 %collective-permute-start.8 = (bf16[1,432,384]{2,1,0:T(8,128)(2,1)S(1)}, bf16[1,432,384]{2,1,0:T(8,128)(2,1)S(1)}, u32[]{:S(2)}, u32[]{:S(2)}) collective-permute-start(bf16[1,432,384]{2,1,0:T(8,128)(2,1)S(1)} %get-tuple-element.216), channel_id=1, source_target_pairs={{0,24},{4,28},{8,16},{12,20},{16,8},{20,12},{24,0},{28,4},{1,25},{... | collective-permute-start | bytes 995336 | tf_op jit(solution)/shard_map/ppermute | solution.py:694
  72.8 1.9 %collective-permute-start.9 = (bf16[4,160,384]{2,1,0:T(8,128)(2,1)S(1)}, bf16[4,160,384]{2,1,0:T(8,128)(2,1)S(1)}, u32[]{:S(2)}, u32[]{:S(2)}) collective-permute-start(bf16[4,160,384]{2,1,0:T(8,128)(2,1)S(1)} %get-tuple-element.190), channel_id=1, source_target_pairs={{0,4},{4,0},{8,12},{12,8},{16,20},{20,16},{24,28},{28,24},{1,5},{5... | collective-permute-start | bytes 1474568 | tf_op jit(solution)/shard_map/ppermute | solution.py:916
  73.1 11.2 %collective-permute-start.15 = (bf16[112,384]{1,0:T(8,128)(2,1)S(1)}, bf16[112,384]{1,0:T(8,128)(2,1)S(1)}, u32[]{:S(2)}, u32[]{:S(2)}) collective-permute-start(bf16[112,384]{1,0:T(8,128)(2,1)S(1)} %pad_maximum_fusion.4), channel_id=1, source_target_pairs={{0,3},{1,2},{2,1},{3,0},{4,7},{5,6},{6,5},{7,4},{8,11},{9,10},{10,... | collective-permute-start | bytes 258056 | tf_op jit(solution)/shard_map/ppermute | solution.py:894
  74.9 5.6 %collective-permute-start.10 = (bf16[1,160,384]{2,1,0:T(8,128)(2,1)S(1)}, bf16[1,160,384]{2,1,0:T(8,128)(2,1)S(1)}, u32[]{:S(2)}, u32[]{:S(2)}) collective-permute-start(bf16[1,160,384]{2,1,0:T(8,128)(2,1)S(1)} %get-tuple-element.220), channel_id=1, source_target_pairs={{0,8},{4,12},{8,0},{12,4},{16,24},{20,28},{24,16},{28,20},{1,9},{5... | collective-permute-start | bytes 368648 | tf_op jit(solution)/shard_map/ppermute | solution.py:694
  76.5 7.7 %collective-permute-start.11 = (bf16[1,160,384]{2,1,0:T(8,128)(2,1)S(1)}, bf16[1,160,384]{2,1,0:T(8,128)(2,1)S(1)}, u32[]{:S(2)}, u32[]{:S(2)}) collective-permute-start(bf16[1,160,384]{2,1,0:T(8,128)(2,1)S(1)} %get-tuple-element.222), channel_id=1, source_target_pairs={{0,16},{4,20},{8,24},{12,28},{16,0},{20,4},{24,8},{28,12},{1,17},{... | collective-permute-start | bytes 368648 | tf_op jit(solution)/shard_map/ppermute | solution.py:694
  78.0 6.2 %collective-permute-start.12 = (bf16[1,160,384]{2,1,0:T(8,128)(2,1)S(1)}, bf16[1,160,384]{2,1,0:T(8,128)(2,1)S(1)}, u32[]{:S(2)}, u32[]{:S(2)}) collective-permute-start(bf16[1,160,384]{2,1,0:T(8,128)(2,1)S(1)} %get-tuple-element.221), channel_id=1, source_target_pairs={{0,24},{4,28},{8,16},{12,20},{16,8},{20,12},{24,0},{28,4},{1,25},{... | collective-permute-start | bytes 368648 | tf_op jit(solution)/shard_map/ppermute | solution.py:694
  78.5 5.8 %collective-permute-start.14 = (bf16[112,384]{1,0:T(8,128)(2,1)S(1)}, bf16[112,384]{1,0:T(8,128)(2,1)S(1)}, u32[]{:S(2)}, u32[]{:S(2)}) collective-permute-start(bf16[112,384]{1,0:T(8,128)(2,1)S(1)} %pad_maximum_fusion.3), channel_id=1, source_target_pairs={{0,2},{1,3},{2,0},{3,1},{4,6},{5,7},{6,4},{7,5},{8,10},{9,11},{10,... | collective-permute-start | bytes 258056 | tf_op jit(solution)/shard_map/ppermute | solution.py:894
  80.5 4.6 %collective-permute-start.13 = (bf16[112,384]{1,0:T(8,128)(2,1)S(1)}, bf16[112,384]{1,0:T(8,128)(2,1)S(1)}, u32[]{:S(2)}, u32[]{:S(2)}) collective-permute-start(bf16[112,384]{1,0:T(8,128)(2,1)S(1)} %pad_maximum_fusion.2), channel_id=1, source_target_pairs={{0,1},{1,0},{2,3},{3,2},{4,5},{5,4},{6,7},{7,6},{8,9},{9,8},{10,11... | collective-permute-start | bytes 258056 | tf_op jit(solution)/shard_map/ppermute | solution.py:894
  85.2 6.2 %collective-permute-start.16 = (bf16[176,384]{1,0:T(8,128)(2,1)S(1)}, bf16[176,384]{1,0:T(8,128)(2,1)S(1)}, u32[]{:S(2)}, u32[]{:S(2)}) collective-permute-start(bf16[176,384]{1,0:T(8,128)(2,1)S(1)} %pad_maximum_fusion.1), channel_id=1, source_target_pairs={{0,1},{1,0},{2,3},{3,2},{4,5},{5,4},{6,7},{7,6},{8,9},{9,8},{10,11... | collective-permute-start | bytes 405512 | tf_op jit(solution)/shard_map/ppermute | solution.py:922
  86.7 11.9 %collective-permute-start.17 = (bf16[176,384]{1,0:T(8,128)(2,1)S(1)}, bf16[176,384]{1,0:T(8,128)(2,1)S(1)}, u32[]{:S(2)}, u32[]{:S(2)}) collective-permute-start(bf16[176,384]{1,0:T(8,128)(2,1)S(1)} %pad_maximum_fusion.1), channel_id=1, source_target_pairs={{0,2},{1,3},{2,0},{3,1},{4,6},{5,7},{6,4},{7,5},{8,10},{9,11},{10,... | collective-permute-start | bytes 405512 | tf_op jit(solution)/shard_map/ppermute | solution.py:922
  88.7 9.9 %collective-permute-start.18 = (bf16[176,384]{1,0:T(8,128)(2,1)S(1)}, bf16[176,384]{1,0:T(8,128)(2,1)S(1)}, u32[]{:S(2)}, u32[]{:S(2)}) collective-permute-start(bf16[176,384]{1,0:T(8,128)(2,1)S(1)} %pad_maximum_fusion.1), channel_id=1, source_target_pairs={{0,3},{1,2},{2,1},{3,0},{4,7},{5,6},{6,5},{7,4},{8,11},{9,10},{10,... | collective-permute-start | bytes 405512 | tf_op jit(solution)/shard_map/ppermute | solution.py:922
where the time goes:
time: 99.9 us; the launch traced here: 99.8 us
  Pallas kernels  60.9 us (61%)
  starting transfers between devices  23.1 us (23%)
  waiting for transfers between devices  12.7 us (13%)
  between operations  1.91 us (2%)
    pallas_call x10, Pallas kernels, call(): pl.pallas_call(kernel, grid=grid, in_specs=in_specs, out_specs=out_specs,...  60.9 us
    ppermute x3, waiting for transfers between devices, per_device(): got = [lax.ppermute(payload, 'mp', xor_perm(mp, j)) for j in range(1, mp)]  8.97 us
    ppermute x6, starting transfers between devices, dp_scatter(): lax.ppermute(value[:, j].astype(BF), 'dp', xor_perm(dp, j << at))  7.11 us
    ppermute x2, starting transfers between devices, per_device(): near = [lax.ppermute(other, 'mp', xor_perm(mp, j)) for j in (1, 2)]  5.68 us
    ppermute x3, starting transfers between devices, per_device(): lax.ppermute(jnp.concatenate([low[2 * j * block:2 * (j + 1) * block], pro...  4.48 us
    ppermute x3, starting transfers between devices, per_device(): got = [lax.ppermute(payload, 'mp', xor_perm(mp, j)) for j in range(1, mp)]  4.45 us
    ppermute x6, waiting for transfers between devices, dp_scatter(): lax.ppermute(value[:, j].astype(BF), 'dp', xor_perm(dp, j << at))  2.64 us
  transfers between devices with their start and end apart: 19, of which 6 were waited for; matrix products, arithmetic and copies ran while one was open for 0% of the time, Pallas kernels for 45%

commit v1 on v0

--- a/solution.py
+++ b/solution.py
@@ -9,6 +9,7 @@
 
 BF = jnp.bfloat16
 F32 = jnp.float32
+LOG2E = 1.4426950408889634
 EPS = 1e-06
 VMEM_LIMIT = 20 * 1024 * 1024
 
@@ -61,7 +62,7 @@
 
 
 def gelu_parts(z):
-    e = jnp.exp(z * z * -0.5)
+    e = jnp.exp2(z * z * (-0.5 * LOG2E))
     t = pl.reciprocal(1.0 + jnp.abs(z) * (0.3275911 * 0.7071067811865476), approx=True)
     poly = t * (
         0.5 * 0.254829592
@@ -121,7 +122,11 @@
 def attn_fwd_kernel(first, share, *refs):
     counts, post_s, postb_s, tok, og, n1g, n1b, qkvb, pre, post, postb, projb = refs[:12]
     gamma1, n2g, n2b, wqkv, wproj = refs[12:17]
-    a1_o, q_o, k_o, v_o, p_o, o_o, x1_o, u_o, a2_o, dy_o, mpre, mpost, mixb = refs[-19:-6]
+    if first:
+        mpre = refs[17]
+        a1_o, q_o, k_o, v_o, p_o, o_o, x1_o, u_o, a2_o, dy_o = refs[-16:-6]
+    else:
+        a1_o, q_o, k_o, v_o, p_o, o_o, x1_o, u_o, a2_o, dy_o, mpre, mpost, mixb = refs[-19:-6]
     pad, kk, attended_t, wide, logits, mixed = refs[-6:]
     images, patches, feats = tok.shape
     rows = pad.shape[0]
@@ -129,13 +134,14 @@
     head_dim = feats // heads
     slots = q_o.shape[1]
 
-    spread = (
-        head_of_lane((heads, feats), 1, head_dim)
-        == lax.broadcasted_iota(jnp.int32, (heads, feats), 0)
-    ).astype(F32)
-    mpre[...] = exact(pre[...], spread, ((1,), (0,))) * head_dim**-0.5
-    mpost[...] = exact(post[...], spread, ((0,), (0,)))
-    mixb[...] = exact(row(postb), spread, ((1,), (0,)))
+    if not first:
+        spread = (
+            head_of_lane((heads, feats), 1, head_dim)
+            == lax.broadcasted_iota(jnp.int32, (heads, feats), 0)
+        ).astype(F32)
+        mpre[...] = exact(pre[...], spread, ((1,), (0,))) * (head_dim**-0.5 * LOG2E)
+        mpost[...] = exact(post[...], spread, ((0,), (0,)))
+        mixb[...] = exact(row(postb), spread, ((1,), (0,)))
 
     @pl.loop(first, first + share)
     def _(i):
@@ -182,7 +188,7 @@
             for lane in range(0, slots, 128):
                 x = logits[g * rows : (g + 1) * rows, lane : lane + 128]
                 x = jnp.concatenate([x[0:tail], jnp.where(inside, x[tail:], -1e30)], axis=0)
-                e = jnp.exp(x - jnp.max(x, axis=0, keepdims=True))
+                e = jnp.exp2(x - jnp.max(x, axis=0, keepdims=True))
                 inv = 1.0 / jnp.sum(e, axis=0, keepdims=True)
                 p_o[i, g, :, lane : lane + 128] = (e * inv).astype(BF)
             mixed[g] = nn(vt, p_o[i, g])
@@ -499,7 +505,7 @@
                 this = dks[h * rows + c.start : h * rows + c.stop, :]
                 dk = dk + this * mpre[h : h + 1, :]
                 sums[h] = sums[h] + fold(kf * this)
-            low = dk.astype(BF)
+            low = (dk * (1.0 / LOG2E)).astype(BF)
             dqkv_o[i, c, feats : 2 * feats] = low
             dk_sum = dk_sum + fold(low.astype(F32))
         for h in range(heads):
@@ -733,24 +739,25 @@
     near = [lax.ppermute(other, "mp", xor_perm(mp, j)) for j in (1, 2)]
 
     shares = [images - 1, 1] if images > 1 else [images]
+    tables = [sds(mix_shape, F32), sds(mix_shape, F32), sds((1, feats), F32)]
     carried = []
     for s, share in enumerate(shares):
         first = sum(shares[:s])
-        ins = [image_counts, mix_post, mix_post_bias] + held
+        ins = [image_counts, mix_post, mix_post_bias] + held + ([mpre] if first else [])
         outs = call(
             functools.partial(attn_fwd_kernel, first, share),
             (),
             ins + carried,
             [SCALARS] * 3
-            + [IN_VMEM] * 14
+            + [IN_VMEM] * (len(ins) - 3)
             + [pl.BlockSpec(memory_space=pl.ANY)] * len(carried),
             [
                 sds(tok_rows, BF), sds(slot_rows, BF), sds(tok_rows, BF), sds(tok_rows, BF),
                 sds(prob_shape, BF), sds(tok_rows, BF), sds(tok_rows, F32), sds(tok_rows, F32),
-                sds(tok_rows, BF), sds(tok_rows, BF), sds(mix_shape, F32), sds(mix_shape, F32),
-                sds((1, feats), F32),
-            ],
-            [IN_VMEM] * 13,
+                sds(tok_rows, BF), sds(tok_rows, BF),
+            ]
+            + ([] if first else tables),
+            [IN_VMEM] * (10 if first else 13),
             [
                 pltpu.VMEM((rows, feats), F32), pltpu.VMEM((heads * rows, 2 * feats), BF),
                 pltpu.VMEM((feats, slots), BF), pltpu.VMEM((rows, 3 * feats), F32), pltpu.VMEM((heads * rows, slots), F32),
@@ -760,7 +767,9 @@
             name="attn_fwd",
             aliases={len(ins) + j: j for j in range(10)} if carried else None,
         )
-        carried, (mpre, mpost, mixb) = list(outs[:10]), outs[10:]
+        carried = list(outs[:10])
+        if not first:
+            mpre, mpost, mixb = outs[10:]
         if s == 0:
             near, carried[0] = lax.optimization_barrier((near, carried[0]))
             last = lax.ppermute(near[1], "mp", xor_perm(mp, 1))

time: 99.9 us -> 99.2 us (level)
  no operation moved by 1% of the time
where the time goes in v1:
time: 99.2 us; the launch traced here: 99.1 us
  Pallas kernels  60.2 us (61%)
  starting transfers between devices  23 us (23%)
  waiting for transfers between devices  12.8 us (13%)
  between operations  1.94 us (2%)
    pallas_call x10, Pallas kernels, call(): pl.pallas_call(kernel, grid=grid, in_specs=in_specs, out_specs=out_specs,...  60.2 us
    ppermute x3, waiting for transfers between devices, per_device(): got = [lax.ppermute(payload, 'mp', xor_perm(mp, j)) for j in range(1, mp)]  9.01 us
    ppermute x6, starting transfers between devices, dp_scatter(): lax.ppermute(value[:, j].astype(BF), 'dp', xor_perm(dp, j << at))  7.11 us
    ppermute x2, starting transfers between devices, per_device(): near = [lax.ppermute(other, 'mp', xor_perm(mp, j)) for j in (1, 2)]  5.68 us
    ppermute x3, starting transfers between devices, per_device(): lax.ppermute(jnp.concatenate([low[2 * j * block:2 * (j + 1) * block], pro...  4.48 us
    ppermute x3, starting transfers between devices, per_device(): got = [lax.ppermute(payload, 'mp', xor_perm(mp, j)) for j in range(1, mp)]  4.45 us
    ppermute x6, waiting for transfers between devices, dp_scatter(): lax.ppermute(value[:, j].astype(BF), 'dp', xor_perm(dp, j << at))  2.65 us
  transfers between devices with their start and end apart: 19, of which 6 were waited for; matrix products, arithmetic and copies ran while one was open for 0% of the time, Pallas kernels for 45%

profile of v1, /device:TPU:0, one launch (start us, length us, event | category | flops | bytes accessed | tf_op | source)
XLA Modules:
  0.0 99.1 jit_solution(1679291857107710122)
XLA Ops:
  0.7 2.2 %pack.1 = (bf16[400,384]{1,0:T(8,128)(2,1)S(1)}, bf16[6,196,384]{2,1,0:T(8,128)(2,1)S(1)}, bf16[6,196,384]{2,1,0:T(8,128)(2,1)S(1)}, f32[384]{0:T(512)S(1)}, f32...) custom-call(bf16[384,384]{1,0:T(8,128)(2,1)} %w1_own.1, ...), custom_call_target="tpu_custom_call" | custom-call | bytes 6899264 | tf_op jit(solution)/shard_map/pack/pallas_call | solution.py:664
  2.9 3.1 %collective-permute-start = (bf16[400,384]{1,0:T(8,128)(2,1)S(1)}, bf16[400,384]{1,0:T(8,128)(2,1)S(1)}, u32[]{:S(2)}, u32[]{:S(2)}) collective-permute-start(bf16[400,384]{1,0:T(8,128)(2,1)S(1)} %get-tuple-element.116), channel_id=1, source_target_pairs={{0,1},{1,0},{2,3},{3,2},{4,5},{5,4},{6,7},{7,6},{8,9},{9,8},{10,11... | collective-permute-start | bytes 921608 | tf_op jit(solution)/shard_map/ppermute | solution.py:739
  6.0 2.6 %collective-permute-start.1 = (bf16[400,384]{1,0:T(8,128)(2,1)S(1)}, bf16[400,384]{1,0:T(8,128)(2,1)S(1)}, u32[]{:S(2)}, u32[]{:S(2)}) collective-permute-start(bf16[400,384]{1,0:T(8,128)(2,1)S(1)} %get-tuple-element.116), channel_id=1, source_target_pairs={{0,2},{1,3},{2,0},{3,1},{4,6},{5,7},{6,4},{7,5},{8,10},{9,11},{10,... | collective-permute-start | bytes 921608 | tf_op jit(solution)/shard_map/ppermute | solution.py:739
  9.2 14.3 %attn_fwd.2 = (bf16[6,208,384]{2,1,0:T(8,128)(2,1)S(1)}, bf16[6,256,384]{2,1,0:T(8,128)(2,1)S(1)}, bf16[6,208,384]{2,1,0:T(8,128)(2,1)S(1)}, bf16[6,208,384]{2,1...) custom-call(s32[1]{0:T(128)S(6)} %copy.61.refs_0_.counts, ...), custom_call_target="tpu_custom_call" | custom-call | flops 7500000256 | bytes 18902852 | tf_op jit(solution)/shard_map/attn_fwd/pallas_call | solution.py:664
  23.5 0.0 collective-permute-done
  23.6 0.0 collective-permute-done.1
  23.6 0.1 pad_maximum_fusion.near
  23.6 0.1 collective-permute-start.2
  23.7 0.5 collective-permute-start.3
  24.2 3.3 %attn_fwd.3 = (bf16[6,208,384]{2,1,0:T(8,128)(2,1)S(1)}, bf16[6,256,384]{2,1,0:T(8,128)(2,1)S(1)}, bf16[6,208,384]{2,1,0:T(8,128)(2,1)S(1)}, bf16[6,208,384]{2,1...) custom-call(s32[1]{0:T(128)S(6)} %copy.61.refs_0_.counts, ...), custom_call_target="tpu_custom_call", output_to_operand_aliasing={{0}: (18, {}), {1}: (19, {}), {2}: (20, {}), {3}: (21, {}),... | custom-call | flops 1500000000 | bytes 34765124 | tf_op jit(solution)/shard_map/attn_fwd/pallas_call | solution.py:664
  27.6 0.0 collective-permute-done.2.far
  27.6 0.0 copy-done.2
  27.6 0.0 copy-done.3
  27.6 0.0 copy-done.9
  27.6 0.0 copy-done.12
  27.6 6.1 %mlp_first.1 = (f32[1248,384]{1,0:T(8,128)S(1)}, f32[1248,384]{1,0:T(8,128)S(1)}, bf16[1248,768]{1,0:T(8,128)(2,1)S(1)}, bf16[1248,768]{1,0:T(8,128)(2,1)S(1)}, bf16[1248,384]{1,0:T(8,128)(2,1)S(1)}) custom-call(bf16[1248,384]{1,0:T(8,128)(2,1)S(1)} %bitcast.67, bf16[1248,384]{1,0:T(8,128)(2,1)S(1)} %bitcast.70, f32[384]{0:T(512)S(1)} %copy-done.12, ...), custom_call_target="tpu_custom_call" | custom-call | flops 3000000000 | bytes 12364800 | tf_op jit(solution)/shard_map/mlp_first/pallas_call | solution.py:664
  33.7 0.0 collective-permute-done.3.last
  33.8 0.2 collective-permute-start.4
  34.0 1.8 %mlp_grad.1 = (bf16[2,768,384]{2,1,0:T(8,128)(2,1)S(1)}, f32[1,768]{1,0:T(1,128)S(1)}, bf16[400,1248]{1,0:T(8,128)(2,1)S(1)}, bf16[384,1248]{1,0:T(8,128)(2,1)S(1)}) custom-call(bf16[1248,384]{1,0:T(8,128)(2,1)S(1)} %bitcast.68, bf16[1248,768]{1,0:T(8,128)(2,1)S(1)} %get-tuple-element.157.hids, bf16[1248,768]{1,0:T(8,128)(2,1)S(1)} %get-tuple-element.158.dzs, ...), custom_call_target="tpu_custom_call" | custom-call | flops 1800000000 | bytes 8890368 | tf_op jit(solution)/shard_map/mlp_grad/pallas_call | solution.py:664
  35.8 0.0 collective-permute-done.4.far_last
  35.8 0.0 copy-done.4
  35.8 0.0 copy-done.10
  35.8 0.0 copy-start
  35.9 0.0 copy-start.1
  35.9 0.0 copy-start.6
  35.9 0.0 copy-start.7
  35.9 11.2 %mlp_rest.1 = (bf16[6,196,384]{2,1,0:T(8,128)(2,1)}, f32[1248,384]{1,0:T(8,128)S(1)}, bf16[6,256,384]{2,1,0:T(8,128)(2,1)S(1)}, bf16[4,432,384]{2,1,0:T(8,128)(2...) custom-call(s32[1]{0:T(128)S(6)} %copy.61.refs_0_.counts, ...), custom_call_target="tpu_custom_call" | custom-call | flops 5400000000 | bytes 23451652 | tf_op jit(solution)/shard_map/mlp_rest/pallas_call | solution.py:664
  47.1 0.4 collective-permute-start.5
  47.5 3.4 %attn_bwd.2 = (bf16[6,208,1152]{2,1,0:T(8,128)(2,1)S(1)}, f32[1,196,384]{2,1,0:T(8,128)S(1)}, f32[32,384]{1,0:T(8,128)S(1)}) custom-call(f32[8,8]{1,0:T(8,128)S(1)} %copy-done.6, bf16[6,256,384]{2,1,0:T(8,128)(2,1)S(1)} %get-tuple-element.175.refs_1_, bf16[6,256,384]{2,1,0:T(8,128)(2,1)S(1)} %get-tuple-element.166.refs_2_, ...), custom_call_target="tpu_custom_call" | custom-call | flops 2000000000 | bytes 16346368 | tf_op jit(solution)/shard_map/attn_bwd/pallas_call | solution.py:664
  50.9 0.0 collective-permute-done.5
  50.9 0.4 fusion.10
  51.3 0.1 slice_bitcast_fusion.3
  51.4 1.6 %collective-permute-start.6 = (bf16[1,432,384]{2,1,0:T(8,128)(2,1)S(1)}, bf16[1,432,384]{2,1,0:T(8,128)(2,1)S(1)}, u32[]{:S(2)}, u32[]{:S(2)}) collective-permute-start(bf16[1,432,384]{2,1,0:T(8,128)(2,1)S(1)} %get-tuple-element.215), channel_id=1, source_target_pairs={{0,8},{4,12},{8,0},{12,4},{16,24},{20,28},{24,16},{28,20},{1,9},{5... | collective-permute-start | bytes 995336 | tf_op jit(solution)/shard_map/ppermute | solution.py:700
  53.0 1.5 %collective-permute-start.7 = (bf16[1,432,384]{2,1,0:T(8,128)(2,1)S(1)}, bf16[1,432,384]{2,1,0:T(8,128)(2,1)S(1)}, u32[]{:S(2)}, u32[]{:S(2)}) collective-permute-start(bf16[1,432,384]{2,1,0:T(8,128)(2,1)S(1)} %get-tuple-element.217), channel_id=1, source_target_pairs={{0,16},{4,20},{8,24},{12,28},{16,0},{20,4},{24,8},{28,12},{1,17},{... | collective-permute-start | bytes 995336 | tf_op jit(solution)/shard_map/ppermute | solution.py:700
  54.5 0.5 collective-permute-start.8
  55.0 15.2 %attn_bwd.3 = (bf16[6,208,1152]{2,1,0:T(8,128)(2,1)S(1)}, f32[6,196,384]{2,1,0:T(8,128)}, f32[32,384]{1,0:T(8,128)S(1)}) custom-call(f32[8,8]{1,0:T(8,128)S(1)} %copy-done.6, bf16[6,256,384]{2,1,0:T(8,128)(2,1)S(1)} %get-tuple-element.175.refs_1_, bf16[6,256,384]{2,1,0:T(8,128)(2,1)S(1)} %get-tuple-element.166.refs_2_, ...), custom_call_target="tpu_custom_call", output_to_operand_aliasing={{0}: (13, {})} | custom-call | flops 10000000000 | bytes 21028096 | tf_op jit(solution)/shard_map/attn_bwd/pallas_call | solution.py:664
  70.2 0.0 collective-permute-done.6
  70.2 0.0 collective-permute-done.7
  70.2 0.0 collective-permute-done.8
  70.2 0.1 fusion.1.refs_3_
  70.4 1.7 %qkv_grad.1 = (bf16[4,160,384]{2,1,0:T(8,128)(2,1)S(1)}, bf16[4,160,384]{2,1,0:T(8,128)(2,1)S(1)}) custom-call(bf16[1248,1152]{1,0:T(8,128)(2,1)S(1)} %bitcast.72, f32[32,384]{1,0:T(8,128)S(1)} %get-tuple-element.183.refs_0_, f32[32,384]{1,0:T(8,128)S(1)} %get-tuple-element.184.refs_1_, bf16[1248,384]{1,0:T(8,128)(2,1)S(1)} %bitcast.65, ...), custom_call_target="tpu_custom_call" | custom-call | flops 1100000000 | bytes 4933632 | tf_op jit(solution)/shard_map/qkv_grad/pallas_call | solution.py:664
  72.1 0.1 collective-permute-start.9
  72.4 1.4 %collective-permute-start.15 = (bf16[112,384]{1,0:T(8,128)(2,1)S(1)}, bf16[112,384]{1,0:T(8,128)(2,1)S(1)}, u32[]{:S(2)}, u32[]{:S(2)}) collective-permute-start(bf16[112,384]{1,0:T(8,128)(2,1)S(1)} %pad_maximum_fusion.4), channel_id=1, source_target_pairs={{0,3},{1,2},{2,1},{3,0},{4,7},{5,6},{6,5},{7,4},{8,11},{9,10},{10,... | collective-permute-start | bytes 258056 | tf_op jit(solution)/shard_map/ppermute | solution.py:903
  73.8 0.3 collective-permute-done.9
  74.1 0.1 fusion.9
  74.2 1.6 %collective-permute-start.10 = (bf16[1,160,384]{2,1,0:T(8,128)(2,1)S(1)}, bf16[1,160,384]{2,1,0:T(8,128)(2,1)S(1)}, u32[]{:S(2)}, u32[]{:S(2)}) collective-permute-start(bf16[1,160,384]{2,1,0:T(8,128)(2,1)S(1)} %get-tuple-element.220), channel_id=1, source_target_pairs={{0,8},{4,12},{8,0},{12,4},{16,24},{20,28},{24,16},{28,20},{1,9},{5... | collective-permute-start | bytes 368648 | tf_op jit(solution)/shard_map/ppermute | solution.py:700
  75.8 1.5 %collective-permute-start.11 = (bf16[1,160,384]{2,1,0:T(8,128)(2,1)S(1)}, bf16[1,160,384]{2,1,0:T(8,128)(2,1)S(1)}, u32[]{:S(2)}, u32[]{:S(2)}) collective-permute-start(bf16[1,160,384]{2,1,0:T(8,128)(2,1)S(1)} %get-tuple-element.222), channel_id=1, source_target_pairs={{0,16},{4,20},{8,24},{12,28},{16,0},{20,4},{24,8},{28,12},{1,17},{... | collective-permute-start | bytes 368648 | tf_op jit(solution)/shard_map/ppermute | solution.py:700
  77.3 0.5 collective-permute-start.12
  77.8 1.5 %collective-permute-start.14 = (bf16[112,384]{1,0:T(8,128)(2,1)S(1)}, bf16[112,384]{1,0:T(8,128)(2,1)S(1)}, u32[]{:S(2)}, u32[]{:S(2)}) collective-permute-start(bf16[112,384]{1,0:T(8,128)(2,1)S(1)} %pad_maximum_fusion.3), channel_id=1, source_target_pairs={{0,2},{1,3},{2,0},{3,1},{4,6},{5,7},{6,4},{7,5},{8,10},{9,11},{10,... | collective-permute-start | bytes 258056 | tf_op jit(solution)/shard_map/ppermute | solution.py:903
  79.3 0.5 collective-permute-done.10
  79.8 1.6 %collective-permute-start.13 = (bf16[112,384]{1,0:T(8,128)(2,1)S(1)}, bf16[112,384]{1,0:T(8,128)(2,1)S(1)}, u32[]{:S(2)}, u32[]{:S(2)}) collective-permute-start(bf16[112,384]{1,0:T(8,128)(2,1)S(1)} %pad_maximum_fusion.2), channel_id=1, source_target_pairs={{0,1},{1,0},{2,3},{3,2},{4,5},{5,4},{6,7},{7,6},{8,9},{9,8},{10,11... | collective-permute-start | bytes 258056 | tf_op jit(solution)/shard_map/ppermute | solution.py:903
  81.4 2.1 %collective-permute-done.11 = bf16[1,160,384]{2,1,0:T(8,128)(2,1)S(1)} collective-permute-done((bf16[1,160,384]{2,1,0:T(8,128)(2,1)S(1)}, bf16[1,160,384]{2,1,0:T(8,128)(2,1)S(1)}, u32[]{:S(2)}, u32[]{:S(2)}) %collective-permute-start.11) | collective-permute-done | bytes 122912 | tf_op jit(solution)/shard_map/ppermute | solution.py:700
  83.5 0.0 collective-permute-done.12
  83.5 0.1 fusion.3.mine
  83.6 0.0 collective-permute-done.15.refs_6_
  83.6 0.0 collective-permute-done.14.refs_5_
  83.6 0.8 collective-permute-done.13.refs_4_
  84.5 1.5 %collective-permute-start.16 = (bf16[176,384]{1,0:T(8,128)(2,1)S(1)}, bf16[176,384]{1,0:T(8,128)(2,1)S(1)}, u32[]{:S(2)}, u32[]{:S(2)}) collective-permute-start(bf16[176,384]{1,0:T(8,128)(2,1)S(1)} %pad_maximum_fusion.1), channel_id=1, source_target_pairs={{0,1},{1,0},{2,3},{3,2},{4,5},{5,4},{6,7},{7,6},{8,9},{9,8},{10,11... | collective-permute-start | bytes 405512 | tf_op jit(solution)/shard_map/ppermute | solution.py:931
  86.0 2.0 %collective-permute-start.17 = (bf16[176,384]{1,0:T(8,128)(2,1)S(1)}, bf16[176,384]{1,0:T(8,128)(2,1)S(1)}, u32[]{:S(2)}, u32[]{:S(2)}) collective-permute-start(bf16[176,384]{1,0:T(8,128)(2,1)S(1)} %pad_maximum_fusion.1), channel_id=1, source_target_pairs={{0,2},{1,3},{2,0},{3,1},{4,6},{5,7},{6,4},{7,5},{8,10},{9,11},{10,... | collective-permute-start | bytes 405512 | tf_op jit(solution)/shard_map/ppermute | solution.py:931
  88.1 0.9 collective-permute-start.18
  88.9 1.8 %collective-permute-done.16.refs_0_ = bf16[176,384]{1,0:T(8,128)(2,1)S(1)} collective-permute-done((bf16[176,384]{1,0:T(8,128)(2,1)S(1)}, bf16[176,384]{1,0:T(8,128)(2,1)S(1)}, u32[]{:S(2)}, u32[]{:S(2)}) %collective-permute-start.16) | collective-permute-done | bytes 135200 | tf_op jit(solution)/shard_map/ppermute | solution.py:931
  90.7 7.2 %collective-permute-done.17.refs_1_ = bf16[176,384]{1,0:T(8,128)(2,1)S(1)} collective-permute-done((bf16[176,384]{1,0:T(8,128)(2,1)S(1)}, bf16[176,384]{1,0:T(8,128)(2,1)S(1)}, u32[]{:S(2)}, u32[]{:S(2)}) %collective-permute-start.17) | collective-permute-done | bytes 135200 | tf_op jit(solution)/shard_map/ppermute | solution.py:931
  98.0 0.0 collective-permute-done.18.refs_2_
  98.0 1.0 final.1
  (29 shorter events, 0.3 us)
Async XLA Ops:
  0.7 8.5 %copy-start.5 = (f32[8,8]{1,0:T(8,128)S(1)}, f32[8,8]{1,0:T(8,128)}, u32[]{:S(2)}) copy-start(f32[8,8]{1,0:T(8,128)} %refs_1_.5) | copy-start | bytes 772
  0.7 8.5 %copy-start.8 = (f32[8]{0:T(128)S(1)}, f32[8]{0:T(128)}, u32[]{:S(2)}) copy-start(f32[8]{0:T(128)} %refs_2_.5) | copy-start | bytes 100
  2.9 20.7 %collective-permute-start = (bf16[400,384]{1,0:T(8,128)(2,1)S(1)}, bf16[400,384]{1,0:T(8,128)(2,1)S(1)}, u32[]{:S(2)}, u32[]{:S(2)}) collective-permute-start(bf16[400,384]{1,0:T(8,128)(2,1)S(1)} %get-tuple-element.116), channel_id=1, source_target_pairs={{0,1},{1,0},{2,3},{3,2},{4,5},{5,4},{6,7},{7,6},{8,9},{9,8},{10,11... | collective-permute-start | bytes 921608 | tf_op jit(solution)/shard_map/ppermute | solution.py:739
  6.0 17.6 %collective-permute-start.1 = (bf16[400,384]{1,0:T(8,128)(2,1)S(1)}, bf16[400,384]{1,0:T(8,128)(2,1)S(1)}, u32[]{:S(2)}, u32[]{:S(2)}) collective-permute-start(bf16[400,384]{1,0:T(8,128)(2,1)S(1)} %get-tuple-element.116), channel_id=1, source_target_pairs={{0,2},{1,3},{2,0},{3,1},{4,6},{5,7},{6,4},{7,5},{8,10},{9,11},{10,... | collective-permute-start | bytes 921608 | tf_op jit(solution)/shard_map/ppermute | solution.py:739
  23.6 3.9 %collective-permute-start.2 = (bf16[2,400,384]{2,1,0:T(8,128)(2,1)S(1)}, bf16[2,400,384]{2,1,0:T(8,128)(2,1)S(1)}, u32[]{:S(2)}, u32[]{:S(2)}) collective-permute-start(bf16[2,400,384]{2,1,0:T(8,128)(2,1)S(1)} %pad_maximum_fusion.near), channel_id=1, source_target_pairs={{0,4},{4,0},{8,12},{12,8},{16,20},{20,16},{24,28},{28,24},{1,5},{5... | collective-permute-start | bytes 1843208 | tf_op jit(solution)/shard_map/ppermute | solution.py:777
  23.7 10.0 %collective-permute-start.3 = (bf16[400,384]{1,0:T(8,128)(2,1)S(1)}, bf16[400,384]{1,0:T(8,128)(2,1)S(1)}, u32[]{:S(2)}, u32[]{:S(2)}) collective-permute-start(bf16[400,384]{1,0:T(8,128)(2,1)S(1)} %collective-permute-done.1), channel_id=1, source_target_pairs={{0,1},{1,0},{2,3},{3,2},{4,5},{5,4},{6,7},{7,6},{8,9},{9,8},{10,11... | collective-permute-start | bytes 921608 | tf_op jit(solution)/shard_map/ppermute | solution.py:775
  24.2 3.4 %copy-start.2 = (bf16[384,384]{1,0:T(8,128)(2,1)S(1)}, bf16[384,384]{1,0:T(8,128)(2,1)}, u32[]{:S(2)}) copy-start(bf16[384,384]{1,0:T(8,128)(2,1)} %w1_own.1) | copy-start | bytes 884740
  24.2 3.4 %copy-start.3 = (bf16[384,384]{1,0:T(8,128)(2,1)S(1)}, bf16[384,384]{1,0:T(8,128)(2,1)}, u32[]{:S(2)}) copy-start(bf16[384,384]{1,0:T(8,128)(2,1)} %w2_own.1) | copy-start | bytes 884740
  24.2 3.4 %copy-start.9 = (f32[384]{0:T(512)S(1)}, f32[384]{0:T(512)}, u32[]{:S(2)}) copy-start(f32[384]{0:T(512)} %b1_own.1) | copy-start | bytes 4612
  24.2 3.4 %copy-start.12 = (f32[384]{0:T(512)S(1)}, f32[384]{0:T(512)}, u32[]{:S(2)}) copy-start(f32[384]{0:T(512)} %gamma2.3) | copy-start | bytes 4612
  33.8 2.0 %collective-permute-start.4 = (bf16[400,384]{1,0:T(8,128)(2,1)S(1)}, bf16[400,384]{1,0:T(8,128)(2,1)S(1)}, u32[]{:S(2)}, u32[]{:S(2)}) collective-permute-start(bf16[400,384]{1,0:T(8,128)(2,1)S(1)} %collective-permute-done.3.last), channel_id=1, source_target_pairs={{0,4},{4,0},{8,12},{12,8},{16,20},{20,16},{24,28},{28,24},{1,5},{5... | collective-permute-start | bytes 921608 | tf_op jit(solution)/shard_map/ppermute | solution.py:808
  34.0 1.8 %copy-start.4 = (bf16[384,384]{1,0:T(8,128)(2,1)S(1)}, bf16[384,384]{1,0:T(8,128)(2,1)}, u32[]{:S(2)}) copy-start(bf16[384,384]{1,0:T(8,128)(2,1)} %wproj.1) | copy-start | bytes 884740
  34.0 1.8 %copy-start.10 = (f32[384]{0:T(512)S(1)}, f32[384]{0:T(512)}, u32[]{:S(2)}) copy-start(f32[384]{0:T(512)} %gamma1.1) | copy-start | bytes 4612
  34.0 1.8 %copy-start.11 = (f32[384]{0:T(512)S(1)}, f32[384]{0:T(512)}, u32[]{:S(2)}) copy-start(f32[384]{0:T(512)} %n2g.1) | copy-start | bytes 4612
  34.0 1.9 %copy-start.13 = (f32[384]{0:T(512)S(1)}, f32[384]{0:T(512)}, u32[]{:S(2)}) copy-start(f32[384]{0:T(512)} %fc2b.1) | copy-start | bytes 4612
  35.8 11.7 %copy-start = (bf16[6,196,384]{2,1,0:T(8,128)(2,1)S(1)}, bf16[6,196,384]{2,1,0:T(8,128)(2,1)}, u32[]{:S(2)}) copy-start(bf16[6,196,384]{2,1,0:T(8,128)(2,1)} %refs_7_.5) | copy-start | bytes 2709508
  35.9 11.6 %copy-start.1 = (bf16[384,1152]{1,0:T(8,128)(2,1)S(1)}, bf16[384,1152]{1,0:T(8,128)(2,1)}, u32[]{:S(2)}) copy-start(bf16[384,1152]{1,0:T(8,128)(2,1)} %refs_11_.5) | copy-start | bytes 2654212
  35.9 11.6 %copy-start.6 = (f32[8,8]{1,0:T(8,128)S(1)}, f32[8,8]{1,0:T(8,128)}, u32[]{:S(2)}) copy-start(f32[8,8]{1,0:T(8,128)} %refs_0_.7) | copy-start | bytes 772
  35.9 11.6 %copy-start.7 = (f32[384]{0:T(512)S(1)}, f32[384]{0:T(512)}, u32[]{:S(2)}) copy-start(f32[384]{0:T(512)} %refs_12_.5) | copy-start | bytes 4612
  47.1 3.9 %collective-permute-start.5 = (bf16[4,432,384]{2,1,0:T(8,128)(2,1)S(1)}, bf16[4,432,384]{2,1,0:T(8,128)(2,1)S(1)}, u32[]{:S(2)}, u32[]{:S(2)}) collective-permute-start(bf16[4,432,384]{2,1,0:T(8,128)(2,1)S(1)} %get-tuple-element.164), channel_id=1, source_target_pairs={{0,4},{4,0},{8,12},{12,8},{16,20},{20,16},{24,28},{28,24},{1,5},{5... | collective-permute-start | bytes 3981320 | tf_op jit(solution)/shard_map/ppermute | solution.py:854
  51.4 18.8 %collective-permute-start.6 = (bf16[1,432,384]{2,1,0:T(8,128)(2,1)S(1)}, bf16[1,432,384]{2,1,0:T(8,128)(2,1)S(1)}, u32[]{:S(2)}, u32[]{:S(2)}) collective-permute-start(bf16[1,432,384]{2,1,0:T(8,128)(2,1)S(1)} %get-tuple-element.215), channel_id=1, source_target_pairs={{0,8},{4,12},{8,0},{12,4},{16,24},{20,28},{24,16},{28,20},{1,9},{5... | collective-permute-start | bytes 995336 | tf_op jit(solution)/shard_map/ppermute | solution.py:700
  53.0 17.2 %collective-permute-start.7 = (bf16[1,432,384]{2,1,0:T(8,128)(2,1)S(1)}, bf16[1,432,384]{2,1,0:T(8,128)(2,1)S(1)}, u32[]{:S(2)}, u32[]{:S(2)}) collective-permute-start(bf16[1,432,384]{2,1,0:T(8,128)(2,1)S(1)} %get-tuple-element.217), channel_id=1, source_target_pairs={{0,16},{4,20},{8,24},{12,28},{16,0},{20,4},{24,8},{28,12},{1,17},{... | collective-permute-start | bytes 995336 | tf_op jit(solution)/shard_map/ppermute | solution.py:700
  54.5 15.7 %collective-permute-start.8 = (bf16[1,432,384]{2,1,0:T(8,128)(2,1)S(1)}, bf16[1,432,384]{2,1,0:T(8,128)(2,1)S(1)}, u32[]{:S(2)}, u32[]{:S(2)}) collective-permute-start(bf16[1,432,384]{2,1,0:T(8,128)(2,1)S(1)} %get-tuple-element.216), channel_id=1, source_target_pairs={{0,24},{4,28},{8,16},{12,20},{16,8},{20,12},{24,0},{28,4},{1,25},{... | collective-permute-start | bytes 995336 | tf_op jit(solution)/shard_map/ppermute | solution.py:700
  72.1 1.9 %collective-permute-start.9 = (bf16[4,160,384]{2,1,0:T(8,128)(2,1)S(1)}, bf16[4,160,384]{2,1,0:T(8,128)(2,1)S(1)}, u32[]{:S(2)}, u32[]{:S(2)}) collective-permute-start(bf16[4,160,384]{2,1,0:T(8,128)(2,1)S(1)} %get-tuple-element.190), channel_id=1, source_target_pairs={{0,4},{4,0},{8,12},{12,8},{16,20},{20,16},{24,28},{28,24},{1,5},{5... | collective-permute-start | bytes 1474568 | tf_op jit(solution)/shard_map/ppermute | solution.py:925
  72.4 11.2 %collective-permute-start.15 = (bf16[112,384]{1,0:T(8,128)(2,1)S(1)}, bf16[112,384]{1,0:T(8,128)(2,1)S(1)}, u32[]{:S(2)}, u32[]{:S(2)}) collective-permute-start(bf16[112,384]{1,0:T(8,128)(2,1)S(1)} %pad_maximum_fusion.4), channel_id=1, source_target_pairs={{0,3},{1,2},{2,1},{3,0},{4,7},{5,6},{6,5},{7,4},{8,11},{9,10},{10,... | collective-permute-start | bytes 258056 | tf_op jit(solution)/shard_map/ppermute | solution.py:903
  74.2 5.6 %collective-permute-start.10 = (bf16[1,160,384]{2,1,0:T(8,128)(2,1)S(1)}, bf16[1,160,384]{2,1,0:T(8,128)(2,1)S(1)}, u32[]{:S(2)}, u32[]{:S(2)}) collective-permute-start(bf16[1,160,384]{2,1,0:T(8,128)(2,1)S(1)} %get-tuple-element.220), channel_id=1, source_target_pairs={{0,8},{4,12},{8,0},{12,4},{16,24},{20,28},{24,16},{28,20},{1,9},{5... | collective-permute-start | bytes 368648 | tf_op jit(solution)/shard_map/ppermute | solution.py:700
  75.8 7.7 %collective-permute-start.11 = (bf16[1,160,384]{2,1,0:T(8,128)(2,1)S(1)}, bf16[1,160,384]{2,1,0:T(8,128)(2,1)S(1)}, u32[]{:S(2)}, u32[]{:S(2)}) collective-permute-start(bf16[1,160,384]{2,1,0:T(8,128)(2,1)S(1)} %get-tuple-element.222), channel_id=1, source_target_pairs={{0,16},{4,20},{8,24},{12,28},{16,0},{20,4},{24,8},{28,12},{1,17},{... | collective-permute-start | bytes 368648 | tf_op jit(solution)/shard_map/ppermute | solution.py:700
  77.3 6.2 %collective-permute-start.12 = (bf16[1,160,384]{2,1,0:T(8,128)(2,1)S(1)}, bf16[1,160,384]{2,1,0:T(8,128)(2,1)S(1)}, u32[]{:S(2)}, u32[]{:S(2)}) collective-permute-start(bf16[1,160,384]{2,1,0:T(8,128)(2,1)S(1)} %get-tuple-element.221), channel_id=1, source_target_pairs={{0,24},{4,28},{8,16},{12,20},{16,8},{20,12},{24,0},{28,4},{1,25},{... | collective-permute-start | bytes 368648 | tf_op jit(solution)/shard_map/ppermute | solution.py:700
  77.8 5.8 %collective-permute-start.14 = (bf16[112,384]{1,0:T(8,128)(2,1)S(1)}, bf16[112,384]{1,0:T(8,128)(2,1)S(1)}, u32[]{:S(2)}, u32[]{:S(2)}) collective-permute-start(bf16[112,384]{1,0:T(8,128)(2,1)S(1)} %pad_maximum_fusion.3), channel_id=1, source_target_pairs={{0,2},{1,3},{2,0},{3,1},{4,6},{5,7},{6,4},{7,5},{8,10},{9,11},{10,... | collective-permute-start | bytes 258056 | tf_op jit(solution)/shard_map/ppermute | solution.py:903
  79.8 4.6 %collective-permute-start.13 = (bf16[112,384]{1,0:T(8,128)(2,1)S(1)}, bf16[112,384]{1,0:T(8,128)(2,1)S(1)}, u32[]{:S(2)}, u32[]{:S(2)}) collective-permute-start(bf16[112,384]{1,0:T(8,128)(2,1)S(1)} %pad_maximum_fusion.2), channel_id=1, source_target_pairs={{0,1},{1,0},{2,3},{3,2},{4,5},{5,4},{6,7},{7,6},{8,9},{9,8},{10,11... | collective-permute-start | bytes 258056 | tf_op jit(solution)/shard_map/ppermute | solution.py:903
  84.5 6.3 %collective-permute-start.16 = (bf16[176,384]{1,0:T(8,128)(2,1)S(1)}, bf16[176,384]{1,0:T(8,128)(2,1)S(1)}, u32[]{:S(2)}, u32[]{:S(2)}) collective-permute-start(bf16[176,384]{1,0:T(8,128)(2,1)S(1)} %pad_maximum_fusion.1), channel_id=1, source_target_pairs={{0,1},{1,0},{2,3},{3,2},{4,5},{5,4},{6,7},{7,6},{8,9},{9,8},{10,11... | collective-permute-start | bytes 405512 | tf_op jit(solution)/shard_map/ppermute | solution.py:931
  86.0 11.9 %collective-permute-start.17 = (bf16[176,384]{1,0:T(8,128)(2,1)S(1)}, bf16[176,384]{1,0:T(8,128)(2,1)S(1)}, u32[]{:S(2)}, u32[]{:S(2)}) collective-permute-start(bf16[176,384]{1,0:T(8,128)(2,1)S(1)} %pad_maximum_fusion.1), channel_id=1, source_target_pairs={{0,2},{1,3},{2,0},{3,1},{4,6},{5,7},{6,4},{7,5},{8,10},{9,11},{10,... | collective-permute-start | bytes 405512 | tf_op jit(solution)/shard_map/ppermute | solution.py:931
  88.1 9.9 %collective-permute-start.18 = (bf16[176,384]{1,0:T(8,128)(2,1)S(1)}, bf16[176,384]{1,0:T(8,128)(2,1)S(1)}, u32[]{:S(2)}, u32[]{:S(2)}) collective-permute-start(bf16[176,384]{1,0:T(8,128)(2,1)S(1)} %pad_maximum_fusion.1), channel_id=1, source_target_pairs={{0,3},{1,2},{2,1},{3,0},{4,7},{5,6},{6,5},{7,4},{8,11},{9,10},{10,... | collective-permute-start | bytes 405512 | tf_op jit(solution)/shard_map/ppermute | solution.py:931

commit v2 on v1

--- a/solution.py
+++ b/solution.py
@@ -175,16 +175,19 @@
                 kk[at, feats:] = (scaled - hi.astype(F32)).astype(BF)
         q2 = jnp.concatenate([q_o[i], q_o[i]], axis=1)
         vt = v_o[i].T
-        many = heads // 2
-        half = many * rows
         tail = patches // 8 * 8
         inside = lax.broadcasted_iota(jnp.int32, (rows - tail, 128), 0) < patches - tail
         real = (lax.broadcasted_iota(jnp.int32, (rows, 128), 0) < patches).astype(BF)
         start = nn(vt, real)
-        for s in range(2):
-            part = slice(s * half, (s + 1) * half)
+
+        def products(pair):
+            part = slice(pair[0] * rows, (pair[1] + 1) * rows)
             logits[part, :] = nt(kk[part, :], q2)
+
+        products((0, 1))
         for g in range(heads):
+            if g % 2 == 0 and g + 2 < heads:
+                products((g + 2, g + 3))
             for lane in range(0, slots, 128):
                 x = logits[g * rows : (g + 1) * rows, lane : lane + 128]
                 x = jnp.concatenate([x[0:tail], jnp.where(inside, x[tail:], -1e30)], axis=0)
@@ -431,17 +434,16 @@
         do_sum = jnp.zeros((8, feats), F32)
         for c in chunks(rows):
             do_sum = do_sum + fold(do_r[i, c, :].astype(F32))
+            vf = v_r[i, c, :].astype(F32)
+            for h in range(heads):
+                at = slice(h * rows + c.start, h * rows + c.stop)
+                vgs[at, :] = (vf * mpost[h : h + 1, :]).astype(BF)
         do_sum = colsum(do_sum)
         q = q_r[i]
         do = do_r[i]
         kt = k_r[i].T
 
         def products(pair):
-            for c in chunks(rows):
-                vf = v_r[i, c, :].astype(F32)
-                for h in pair:
-                    at = slice(h * rows + c.start, h * rows + c.stop)
-                    vgs[at, :] = (vf * mpost[h : h + 1, :]).astype(BF)
             part = slice(pair[0] * rows, (pair[1] + 1) * rows)
             dps[part, :] = nt(vgs[part, :], do)
             dvs[part, :] = nn(p_r[i, pair[0] : pair[1] + 1].reshape(2 * rows, slots), do)

time: 99.2 us -> 100 us (level)
  Pallas kernels: 60.2 us -> 61.3 us
    pallas_call x10, Pallas kernels: 60.2 us -> 61.3 us  [call(): pl.pallas_call(kernel, grid=grid, in_specs=in_specs, out_specs=out_specs,...]
where the time goes in v2:
time: 100 us
  Pallas kernels  61.3 us (61%)
  starting transfers between devices  23 us (23%)
  waiting for transfers between devices  12.8 us (13%)
  between operations  1.93 us (2%)
    pallas_call x10, Pallas kernels, call(): pl.pallas_call(kernel, grid=grid, in_specs=in_specs, out_specs=out_specs,...  61.3 us
    ppermute x3, waiting for transfers between devices, per_device(): got = [lax.ppermute(payload, 'mp', xor_perm(mp, j)) for j in range(1, mp)]  8.98 us
    ppermute x6, starting transfers between devices, dp_scatter(): lax.ppermute(value[:, j].astype(BF), 'dp', xor_perm(dp, j << at))  7.11 us
    ppermute x2, starting transfers between devices, per_device(): near = [lax.ppermute(other, 'mp', xor_perm(mp, j)) for j in (1, 2)]  5.68 us
    ppermute x3, starting transfers between devices, per_device(): lax.ppermute(jnp.concatenate([low[2 * j * block:2 * (j + 1) * block], pro...  4.46 us
    ppermute x3, starting transfers between devices, per_device(): got = [lax.ppermute(payload, 'mp', xor_perm(mp, j)) for j in range(1, mp)]  4.45 us
    ppermute x6, waiting for transfers between devices, dp_scatter(): lax.ppermute(value[:, j].astype(BF), 'dp', xor_perm(dp, j << at))  2.65 us
  transfers between devices with their start and end apart: 19, of which 6 were waited for; matrix products, arithmetic and copies ran while one was open for 0% of the time, Pallas kernels for 45%

profile of v2, /device:TPU:0, one launch (start us, length us, event | category | flops | bytes accessed | tf_op | source)
XLA Modules:
  0.0 100.2 jit_solution(1199751255693468781)
XLA Ops:
  0.7 0.0 copy-start.5
  0.7 0.0 copy-start.8
  0.7 2.2 %pack.1 = (bf16[400,384]{1,0:T(8,128)(2,1)S(1)}, bf16[6,196,384]{2,1,0:T(8,128)(2,1)S(1)}, bf16[6,196,384]{2,1,0:T(8,128)(2,1)S(1)}, f32[384]{0:T(512)S(1)}, f32...) custom-call(bf16[384,384]{1,0:T(8,128)(2,1)} %w1_own.1, ...), custom_call_target="tpu_custom_call" | custom-call | bytes 6899264 | tf_op jit(solution)/shard_map/pack/pallas_call | solution.py:666
  2.9 3.1 %collective-permute-start = (bf16[400,384]{1,0:T(8,128)(2,1)S(1)}, bf16[400,384]{1,0:T(8,128)(2,1)S(1)}, u32[]{:S(2)}, u32[]{:S(2)}) collective-permute-start(bf16[400,384]{1,0:T(8,128)(2,1)S(1)} %get-tuple-element.116), channel_id=1, source_target_pairs={{0,1},{1,0},{2,3},{3,2},{4,5},{5,4},{6,7},{7,6},{8,9},{9,8},{10,11... | collective-permute-start | bytes 921608 | tf_op jit(solution)/shard_map/ppermute | solution.py:741
  6.0 2.6 %collective-permute-start.1 = (bf16[400,384]{1,0:T(8,128)(2,1)S(1)}, bf16[400,384]{1,0:T(8,128)(2,1)S(1)}, u32[]{:S(2)}, u32[]{:S(2)}) collective-permute-start(bf16[400,384]{1,0:T(8,128)(2,1)S(1)} %get-tuple-element.116), channel_id=1, source_target_pairs={{0,2},{1,3},{2,0},{3,1},{4,6},{5,7},{6,4},{7,5},{8,10},{9,11},{10,... | collective-permute-start | bytes 921608 | tf_op jit(solution)/shard_map/ppermute | solution.py:741
  9.2 0.0 copy-done.5
  9.2 0.0 copy-done.8
  9.2 15.5 %attn_fwd.2 = (bf16[6,208,384]{2,1,0:T(8,128)(2,1)S(1)}, bf16[6,256,384]{2,1,0:T(8,128)(2,1)S(1)}, bf16[6,208,384]{2,1,0:T(8,128)(2,1)S(1)}, bf16[6,208,384]{2,1...) custom-call(s32[1]{0:T(128)S(6)} %copy.61.refs_0_.counts, ...), custom_call_target="tpu_custom_call" | custom-call | flops 7500000256 | bytes 18902852 | tf_op jit(solution)/shard_map/attn_fwd/pallas_call | solution.py:666
  24.7 0.0 collective-permute-done
  24.7 0.0 collective-permute-done.1
  24.7 0.1 pad_maximum_fusion.near
  24.8 0.1 collective-permute-start.2
  24.9 0.5 collective-permute-start.3
  25.4 3.6 %attn_fwd.3 = (bf16[6,208,384]{2,1,0:T(8,128)(2,1)S(1)}, bf16[6,256,384]{2,1,0:T(8,128)(2,1)S(1)}, bf16[6,208,384]{2,1,0:T(8,128)(2,1)S(1)}, bf16[6,208,384]{2,1...) custom-call(s32[1]{0:T(128)S(6)} %copy.61.refs_0_.counts, ...), custom_call_target="tpu_custom_call", output_to_operand_aliasing={{0}: (18, {}), {1}: (19, {}), {2}: (20, {}), {3}: (21, {}),... | custom-call | flops 1500000000 | bytes 34765124 | tf_op jit(solution)/shard_map/attn_fwd/pallas_call | solution.py:666
  29.0 0.0 collective-permute-done.2.far
  29.0 0.0 copy-done.2
  29.0 0.0 copy-done.3
  29.0 6.1 %mlp_first.1 = (f32[1248,384]{1,0:T(8,128)S(1)}, f32[1248,384]{1,0:T(8,128)S(1)}, bf16[1248,768]{1,0:T(8,128)(2,1)S(1)}, bf16[1248,768]{1,0:T(8,128)(2,1)S(1)}, bf16[1248,384]{1,0:T(8,128)(2,1)S(1)}) custom-call(bf16[1248,384]{1,0:T(8,128)(2,1)S(1)} %bitcast.67, bf16[1248,384]{1,0:T(8,128)(2,1)S(1)} %bitcast.70, f32[384]{0:T(512)S(1)} %copy-done.12, ...), custom_call_target="tpu_custom_call" | custom-call | flops 3000000000 | bytes 12364800 | tf_op jit(solution)/shard_map/mlp_first/pallas_call | solution.py:666
  35.1 0.0 collective-permute-done.3.last
  35.1 0.2 collective-permute-start.4
  35.4 1.8 %mlp_grad.1 = (bf16[2,768,384]{2,1,0:T(8,128)(2,1)S(1)}, f32[1,768]{1,0:T(1,128)S(1)}, bf16[400,1248]{1,0:T(8,128)(2,1)S(1)}, bf16[384,1248]{1,0:T(8,128)(2,1)S(1)}) custom-call(bf16[1248,384]{1,0:T(8,128)(2,1)S(1)} %bitcast.68, bf16[1248,768]{1,0:T(8,128)(2,1)S(1)} %get-tuple-element.157.hids, bf16[1248,768]{1,0:T(8,128)(2,1)S(1)} %get-tuple-element.158.dzs, ...), custom_call_target="tpu_custom_call" | custom-call | flops 1800000000 | bytes 8890368 | tf_op jit(solution)/shard_map/mlp_grad/pallas_call | solution.py:666
  37.2 0.0 collective-permute-done.4.far_last
  37.2 0.0 copy-start
  37.2 0.0 copy-start.1
  37.3 0.0 copy-start.6
  37.3 0.0 copy-start.7
  37.3 11.2 %mlp_rest.1 = (bf16[6,196,384]{2,1,0:T(8,128)(2,1)}, f32[1248,384]{1,0:T(8,128)S(1)}, bf16[6,256,384]{2,1,0:T(8,128)(2,1)S(1)}, bf16[4,432,384]{2,1,0:T(8,128)(2...) custom-call(s32[1]{0:T(128)S(6)} %copy.61.refs_0_.counts, ...), custom_call_target="tpu_custom_call" | custom-call | flops 5400000000 | bytes 23451652 | tf_op jit(solution)/shard_map/mlp_rest/pallas_call | solution.py:666
  48.4 0.4 collective-permute-start.5
  48.9 3.3 %attn_bwd.2 = (bf16[6,208,1152]{2,1,0:T(8,128)(2,1)S(1)}, f32[1,196,384]{2,1,0:T(8,128)S(1)}, f32[32,384]{1,0:T(8,128)S(1)}) custom-call(f32[8,8]{1,0:T(8,128)S(1)} %copy-done.6, bf16[6,256,384]{2,1,0:T(8,128)(2,1)S(1)} %get-tuple-element.175.refs_1_, bf16[6,256,384]{2,1,0:T(8,128)(2,1)S(1)} %get-tuple-element.166.refs_2_, ...), custom_call_target="tpu_custom_call" | custom-call | flops 2000000000 | bytes 16346368 | tf_op jit(solution)/shard_map/attn_bwd/pallas_call | solution.py:666
  52.2 0.0 collective-permute-done.5
  52.2 0.4 fusion.10
  52.6 0.1 slice_bitcast_fusion.3
  52.7 1.6 %collective-permute-start.6 = (bf16[1,432,384]{2,1,0:T(8,128)(2,1)S(1)}, bf16[1,432,384]{2,1,0:T(8,128)(2,1)S(1)}, u32[]{:S(2)}, u32[]{:S(2)}) collective-permute-start(bf16[1,432,384]{2,1,0:T(8,128)(2,1)S(1)} %get-tuple-element.215), channel_id=1, source_target_pairs={{0,8},{4,12},{8,0},{12,4},{16,24},{20,28},{24,16},{28,20},{1,9},{5... | collective-permute-start | bytes 995336 | tf_op jit(solution)/shard_map/ppermute | solution.py:702
  54.3 1.5 %collective-permute-start.7 = (bf16[1,432,384]{2,1,0:T(8,128)(2,1)S(1)}, bf16[1,432,384]{2,1,0:T(8,128)(2,1)S(1)}, u32[]{:S(2)}, u32[]{:S(2)}) collective-permute-start(bf16[1,432,384]{2,1,0:T(8,128)(2,1)S(1)} %get-tuple-element.217), channel_id=1, source_target_pairs={{0,16},{4,20},{8,24},{12,28},{16,0},{20,4},{24,8},{28,12},{1,17},{... | collective-permute-start | bytes 995336 | tf_op jit(solution)/shard_map/ppermute | solution.py:702
  55.8 0.5 collective-permute-start.8
  56.3 15.0 %attn_bwd.3 = (bf16[6,208,1152]{2,1,0:T(8,128)(2,1)S(1)}, f32[6,196,384]{2,1,0:T(8,128)}, f32[32,384]{1,0:T(8,128)S(1)}) custom-call(f32[8,8]{1,0:T(8,128)S(1)} %copy-done.6, bf16[6,256,384]{2,1,0:T(8,128)(2,1)S(1)} %get-tuple-element.175.refs_1_, bf16[6,256,384]{2,1,0:T(8,128)(2,1)S(1)} %get-tuple-element.166.refs_2_, ...), custom_call_target="tpu_custom_call", output_to_operand_aliasing={{0}: (13, {})} | custom-call | flops 10000000000 | bytes 21028096 | tf_op jit(solution)/shard_map/attn_bwd/pallas_call | solution.py:666
  71.3 0.0 collective-permute-done.6
  71.3 0.0 collective-permute-done.7
  71.3 0.0 collective-permute-done.8
  71.3 0.1 fusion.1.refs_3_
  71.5 1.7 %qkv_grad.1 = (bf16[4,160,384]{2,1,0:T(8,128)(2,1)S(1)}, bf16[4,160,384]{2,1,0:T(8,128)(2,1)S(1)}) custom-call(bf16[1248,1152]{1,0:T(8,128)(2,1)S(1)} %bitcast.72, f32[32,384]{1,0:T(8,128)S(1)} %get-tuple-element.183.refs_0_, f32[32,384]{1,0:T(8,128)S(1)} %get-tuple-element.184.refs_1_, bf16[1248,384]{1,0:T(8,128)(2,1)S(1)} %bitcast.65, ...), custom_call_target="tpu_custom_call" | custom-call | flops 1100000000 | bytes 4933632 | tf_op jit(solution)/shard_map/qkv_grad/pallas_call | solution.py:666
  73.2 0.1 collective-permute-start.9
  73.5 1.4 %collective-permute-start.15 = (bf16[112,384]{1,0:T(8,128)(2,1)S(1)}, bf16[112,384]{1,0:T(8,128)(2,1)S(1)}, u32[]{:S(2)}, u32[]{:S(2)}) collective-permute-start(bf16[112,384]{1,0:T(8,128)(2,1)S(1)} %pad_maximum_fusion.4), channel_id=1, source_target_pairs={{0,3},{1,2},{2,1},{3,0},{4,7},{5,6},{6,5},{7,4},{8,11},{9,10},{10,... | collective-permute-start | bytes 258056 | tf_op jit(solution)/shard_map/ppermute | solution.py:905
  74.9 0.3 collective-permute-done.9
  75.2 0.1 fusion.9
  75.3 1.6 %collective-permute-start.10 = (bf16[1,160,384]{2,1,0:T(8,128)(2,1)S(1)}, bf16[1,160,384]{2,1,0:T(8,128)(2,1)S(1)}, u32[]{:S(2)}, u32[]{:S(2)}) collective-permute-start(bf16[1,160,384]{2,1,0:T(8,128)(2,1)S(1)} %get-tuple-element.220), channel_id=1, source_target_pairs={{0,8},{4,12},{8,0},{12,4},{16,24},{20,28},{24,16},{28,20},{1,9},{5... | collective-permute-start | bytes 368648 | tf_op jit(solution)/shard_map/ppermute | solution.py:702
  76.9 1.5 %collective-permute-start.11 = (bf16[1,160,384]{2,1,0:T(8,128)(2,1)S(1)}, bf16[1,160,384]{2,1,0:T(8,128)(2,1)S(1)}, u32[]{:S(2)}, u32[]{:S(2)}) collective-permute-start(bf16[1,160,384]{2,1,0:T(8,128)(2,1)S(1)} %get-tuple-element.222), channel_id=1, source_target_pairs={{0,16},{4,20},{8,24},{12,28},{16,0},{20,4},{24,8},{28,12},{1,17},{... | collective-permute-start | bytes 368648 | tf_op jit(solution)/shard_map/ppermute | solution.py:702
  78.4 0.5 collective-permute-start.12
  78.9 1.5 %collective-permute-start.14 = (bf16[112,384]{1,0:T(8,128)(2,1)S(1)}, bf16[112,384]{1,0:T(8,128)(2,1)S(1)}, u32[]{:S(2)}, u32[]{:S(2)}) collective-permute-start(bf16[112,384]{1,0:T(8,128)(2,1)S(1)} %pad_maximum_fusion.3), channel_id=1, source_target_pairs={{0,2},{1,3},{2,0},{3,1},{4,6},{5,7},{6,4},{7,5},{8,10},{9,11},{10,... | collective-permute-start | bytes 258056 | tf_op jit(solution)/shard_map/ppermute | solution.py:905
  80.4 0.5 collective-permute-done.10
  80.9 1.6 %collective-permute-start.13 = (bf16[112,384]{1,0:T(8,128)(2,1)S(1)}, bf16[112,384]{1,0:T(8,128)(2,1)S(1)}, u32[]{:S(2)}, u32[]{:S(2)}) collective-permute-start(bf16[112,384]{1,0:T(8,128)(2,1)S(1)} %pad_maximum_fusion.2), channel_id=1, source_target_pairs={{0,1},{1,0},{2,3},{3,2},{4,5},{5,4},{6,7},{7,6},{8,9},{9,8},{10,11... | collective-permute-start | bytes 258056 | tf_op jit(solution)/shard_map/ppermute | solution.py:905
  82.5 2.1 %collective-permute-done.11 = bf16[1,160,384]{2,1,0:T(8,128)(2,1)S(1)} collective-permute-done((bf16[1,160,384]{2,1,0:T(8,128)(2,1)S(1)}, bf16[1,160,384]{2,1,0:T(8,128)(2,1)S(1)}, u32[]{:S(2)}, u32[]{:S(2)}) %collective-permute-start.11) | collective-permute-done | bytes 122912 | tf_op jit(solution)/shard_map/ppermute | solution.py:702
  84.6 0.0 collective-permute-done.12
  84.6 0.1 fusion.3.mine
  84.7 0.0 collective-permute-done.15.refs_6_
  84.7 0.0 collective-permute-done.14.refs_5_
  84.7 0.8 collective-permute-done.13.refs_4_
  85.6 1.5 %collective-permute-start.16 = (bf16[176,384]{1,0:T(8,128)(2,1)S(1)}, bf16[176,384]{1,0:T(8,128)(2,1)S(1)}, u32[]{:S(2)}, u32[]{:S(2)}) collective-permute-start(bf16[176,384]{1,0:T(8,128)(2,1)S(1)} %pad_maximum_fusion.1), channel_id=1, source_target_pairs={{0,1},{1,0},{2,3},{3,2},{4,5},{5,4},{6,7},{7,6},{8,9},{9,8},{10,11... | collective-permute-start | bytes 405512 | tf_op jit(solution)/shard_map/ppermute | solution.py:933
  87.1 2.0 %collective-permute-start.17 = (bf16[176,384]{1,0:T(8,128)(2,1)S(1)}, bf16[176,384]{1,0:T(8,128)(2,1)S(1)}, u32[]{:S(2)}, u32[]{:S(2)}) collective-permute-start(bf16[176,384]{1,0:T(8,128)(2,1)S(1)} %pad_maximum_fusion.1), channel_id=1, source_target_pairs={{0,2},{1,3},{2,0},{3,1},{4,6},{5,7},{6,4},{7,5},{8,10},{9,11},{10,... | collective-permute-start | bytes 405512 | tf_op jit(solution)/shard_map/ppermute | solution.py:933
  89.2 0.9 collective-permute-start.18
  90.1 1.8 %collective-permute-done.16.refs_0_ = bf16[176,384]{1,0:T(8,128)(2,1)S(1)} collective-permute-done((bf16[176,384]{1,0:T(8,128)(2,1)S(1)}, bf16[176,384]{1,0:T(8,128)(2,1)S(1)}, u32[]{:S(2)}, u32[]{:S(2)}) %collective-permute-start.16) | collective-permute-done | bytes 135200 | tf_op jit(solution)/shard_map/ppermute | solution.py:933
  91.8 7.2 %collective-permute-done.17.refs_1_ = bf16[176,384]{1,0:T(8,128)(2,1)S(1)} collective-permute-done((bf16[176,384]{1,0:T(8,128)(2,1)S(1)}, bf16[176,384]{1,0:T(8,128)(2,1)S(1)}, u32[]{:S(2)}, u32[]{:S(2)}) %collective-permute-start.17) | collective-permute-done | bytes 135200 | tf_op jit(solution)/shard_map/ppermute | solution.py:933
  99.0 0.0 collective-permute-done.18.refs_2_
  99.0 1.0 final.1
  (29 shorter events, 0.3 us)
Async XLA Ops:
  0.7 8.5 %copy-start.5 = (f32[8,8]{1,0:T(8,128)S(1)}, f32[8,8]{1,0:T(8,128)}, u32[]{:S(2)}) copy-start(f32[8,8]{1,0:T(8,128)} %refs_1_.5) | copy-start | bytes 772
  0.7 8.5 %copy-start.8 = (f32[8]{0:T(128)S(1)}, f32[8]{0:T(128)}, u32[]{:S(2)}) copy-start(f32[8]{0:T(128)} %refs_2_.5) | copy-start | bytes 100
  2.9 21.8 %collective-permute-start = (bf16[400,384]{1,0:T(8,128)(2,1)S(1)}, bf16[400,384]{1,0:T(8,128)(2,1)S(1)}, u32[]{:S(2)}, u32[]{:S(2)}) collective-permute-start(bf16[400,384]{1,0:T(8,128)(2,1)S(1)} %get-tuple-element.116), channel_id=1, source_target_pairs={{0,1},{1,0},{2,3},{3,2},{4,5},{5,4},{6,7},{7,6},{8,9},{9,8},{10,11... | collective-permute-start | bytes 921608 | tf_op jit(solution)/shard_map/ppermute | solution.py:741
  6.0 18.7 %collective-permute-start.1 = (bf16[400,384]{1,0:T(8,128)(2,1)S(1)}, bf16[400,384]{1,0:T(8,128)(2,1)S(1)}, u32[]{:S(2)}, u32[]{:S(2)}) collective-permute-start(bf16[400,384]{1,0:T(8,128)(2,1)S(1)} %get-tuple-element.116), channel_id=1, source_target_pairs={{0,2},{1,3},{2,0},{3,1},{4,6},{5,7},{6,4},{7,5},{8,10},{9,11},{10,... | collective-permute-start | bytes 921608 | tf_op jit(solution)/shard_map/ppermute | solution.py:741
  24.8 4.2 %collective-permute-start.2 = (bf16[2,400,384]{2,1,0:T(8,128)(2,1)S(1)}, bf16[2,400,384]{2,1,0:T(8,128)(2,1)S(1)}, u32[]{:S(2)}, u32[]{:S(2)}) collective-permute-start(bf16[2,400,384]{2,1,0:T(8,128)(2,1)S(1)} %pad_maximum_fusion.near), channel_id=1, source_target_pairs={{0,4},{4,0},{8,12},{12,8},{16,20},{20,16},{24,28},{28,24},{1,5},{5... | collective-permute-start | bytes 1843208 | tf_op jit(solution)/shard_map/ppermute | solution.py:779
  24.9 10.3 %collective-permute-start.3 = (bf16[400,384]{1,0:T(8,128)(2,1)S(1)}, bf16[400,384]{1,0:T(8,128)(2,1)S(1)}, u32[]{:S(2)}, u32[]{:S(2)}) collective-permute-start(bf16[400,384]{1,0:T(8,128)(2,1)S(1)} %collective-permute-done.1), channel_id=1, source_target_pairs={{0,1},{1,0},{2,3},{3,2},{4,5},{5,4},{6,7},{7,6},{8,9},{9,8},{10,11... | collective-permute-start | bytes 921608 | tf_op jit(solution)/shard_map/ppermute | solution.py:777
  25.4 3.6 %copy-start.2 = (bf16[384,384]{1,0:T(8,128)(2,1)S(1)}, bf16[384,384]{1,0:T(8,128)(2,1)}, u32[]{:S(2)}) copy-start(bf16[384,384]{1,0:T(8,128)(2,1)} %w1_own.1) | copy-start | bytes 884740
  25.4 3.6 %copy-start.3 = (bf16[384,384]{1,0:T(8,128)(2,1)S(1)}, bf16[384,384]{1,0:T(8,128)(2,1)}, u32[]{:S(2)}) copy-start(bf16[384,384]{1,0:T(8,128)(2,1)} %w2_own.1) | copy-start | bytes 884740
  25.4 3.6 %copy-start.9 = (f32[384]{0:T(512)S(1)}, f32[384]{0:T(512)}, u32[]{:S(2)}) copy-start(f32[384]{0:T(512)} %b1_own.1) | copy-start | bytes 4612
  25.4 3.6 %copy-start.12 = (f32[384]{0:T(512)S(1)}, f32[384]{0:T(512)}, u32[]{:S(2)}) copy-start(f32[384]{0:T(512)} %gamma2.3) | copy-start | bytes 4612
  35.1 2.0 %collective-permute-start.4 = (bf16[400,384]{1,0:T(8,128)(2,1)S(1)}, bf16[400,384]{1,0:T(8,128)(2,1)S(1)}, u32[]{:S(2)}, u32[]{:S(2)}) collective-permute-start(bf16[400,384]{1,0:T(8,128)(2,1)S(1)} %collective-permute-done.3.last), channel_id=1, source_target_pairs={{0,4},{4,0},{8,12},{12,8},{16,20},{20,16},{24,28},{28,24},{1,5},{5... | collective-permute-start | bytes 921608 | tf_op jit(solution)/shard_map/ppermute | solution.py:810
  35.4 1.8 %copy-start.4 = (bf16[384,384]{1,0:T(8,128)(2,1)S(1)}, bf16[384,384]{1,0:T(8,128)(2,1)}, u32[]{:S(2)}) copy-start(bf16[384,384]{1,0:T(8,128)(2,1)} %wproj.1) | copy-start | bytes 884740
  35.4 1.8 %copy-start.10 = (f32[384]{0:T(512)S(1)}, f32[384]{0:T(512)}, u32[]{:S(2)}) copy-start(f32[384]{0:T(512)} %gamma1.1) | copy-start | bytes 4612
  35.4 1.8 %copy-start.11 = (f32[384]{0:T(512)S(1)}, f32[384]{0:T(512)}, u32[]{:S(2)}) copy-start(f32[384]{0:T(512)} %n2g.1) | copy-start | bytes 4612
  35.4 1.9 %copy-start.13 = (f32[384]{0:T(512)S(1)}, f32[384]{0:T(512)}, u32[]{:S(2)}) copy-start(f32[384]{0:T(512)} %fc2b.1) | copy-start | bytes 4612
  37.2 11.7 %copy-start = (bf16[6,196,384]{2,1,0:T(8,128)(2,1)S(1)}, bf16[6,196,384]{2,1,0:T(8,128)(2,1)}, u32[]{:S(2)}) copy-start(bf16[6,196,384]{2,1,0:T(8,128)(2,1)} %refs_7_.5) | copy-start | bytes 2709508
  37.2 11.6 %copy-start.1 = (bf16[384,1152]{1,0:T(8,128)(2,1)S(1)}, bf16[384,1152]{1,0:T(8,128)(2,1)}, u32[]{:S(2)}) copy-start(bf16[384,1152]{1,0:T(8,128)(2,1)} %refs_11_.5) | copy-start | bytes 2654212
  37.3 11.6 %copy-start.6 = (f32[8,8]{1,0:T(8,128)S(1)}, f32[8,8]{1,0:T(8,128)}, u32[]{:S(2)}) copy-start(f32[8,8]{1,0:T(8,128)} %refs_0_.7) | copy-start | bytes 772
  37.3 11.6 %copy-start.7 = (f32[384]{0:T(512)S(1)}, f32[384]{0:T(512)}, u32[]{:S(2)}) copy-start(f32[384]{0:T(512)} %refs_12_.5) | copy-start | bytes 4612
  48.4 3.8 %collective-permute-start.5 = (bf16[4,432,384]{2,1,0:T(8,128)(2,1)S(1)}, bf16[4,432,384]{2,1,0:T(8,128)(2,1)S(1)}, u32[]{:S(2)}, u32[]{:S(2)}) collective-permute-start(bf16[4,432,384]{2,1,0:T(8,128)(2,1)S(1)} %get-tuple-element.164), channel_id=1, source_target_pairs={{0,4},{4,0},{8,12},{12,8},{16,20},{20,16},{24,28},{28,24},{1,5},{5... | collective-permute-start | bytes 3981320 | tf_op jit(solution)/shard_map/ppermute | solution.py:856
  52.7 18.6 %collective-permute-start.6 = (bf16[1,432,384]{2,1,0:T(8,128)(2,1)S(1)}, bf16[1,432,384]{2,1,0:T(8,128)(2,1)S(1)}, u32[]{:S(2)}, u32[]{:S(2)}) collective-permute-start(bf16[1,432,384]{2,1,0:T(8,128)(2,1)S(1)} %get-tuple-element.215), channel_id=1, source_target_pairs={{0,8},{4,12},{8,0},{12,4},{16,24},{20,28},{24,16},{28,20},{1,9},{5... | collective-permute-start | bytes 995336 | tf_op jit(solution)/shard_map/ppermute | solution.py:702
  54.3 17.1 %collective-permute-start.7 = (bf16[1,432,384]{2,1,0:T(8,128)(2,1)S(1)}, bf16[1,432,384]{2,1,0:T(8,128)(2,1)S(1)}, u32[]{:S(2)}, u32[]{:S(2)}) collective-permute-start(bf16[1,432,384]{2,1,0:T(8,128)(2,1)S(1)} %get-tuple-element.217), channel_id=1, source_target_pairs={{0,16},{4,20},{8,24},{12,28},{16,0},{20,4},{24,8},{28,12},{1,17},{... | collective-permute-start | bytes 995336 | tf_op jit(solution)/shard_map/ppermute | solution.py:702
  55.8 15.5 %collective-permute-start.8 = (bf16[1,432,384]{2,1,0:T(8,128)(2,1)S(1)}, bf16[1,432,384]{2,1,0:T(8,128)(2,1)S(1)}, u32[]{:S(2)}, u32[]{:S(2)}) collective-permute-start(bf16[1,432,384]{2,1,0:T(8,128)(2,1)S(1)} %get-tuple-element.216), channel_id=1, source_target_pairs={{0,24},{4,28},{8,16},{12,20},{16,8},{20,12},{24,0},{28,4},{1,25},{... | collective-permute-start | bytes 995336 | tf_op jit(solution)/shard_map/ppermute | solution.py:702
  73.2 1.9 %collective-permute-start.9 = (bf16[4,160,384]{2,1,0:T(8,128)(2,1)S(1)}, bf16[4,160,384]{2,1,0:T(8,128)(2,1)S(1)}, u32[]{:S(2)}, u32[]{:S(2)}) collective-permute-start(bf16[4,160,384]{2,1,0:T(8,128)(2,1)S(1)} %get-tuple-element.190), channel_id=1, source_target_pairs={{0,4},{4,0},{8,12},{12,8},{16,20},{20,16},{24,28},{28,24},{1,5},{5... | collective-permute-start | bytes 1474568 | tf_op jit(solution)/shard_map/ppermute | solution.py:927
  73.5 11.2 %collective-permute-start.15 = (bf16[112,384]{1,0:T(8,128)(2,1)S(1)}, bf16[112,384]{1,0:T(8,128)(2,1)S(1)}, u32[]{:S(2)}, u32[]{:S(2)}) collective-permute-start(bf16[112,384]{1,0:T(8,128)(2,1)S(1)} %pad_maximum_fusion.4), channel_id=1, source_target_pairs={{0,3},{1,2},{2,1},{3,0},{4,7},{5,6},{6,5},{7,4},{8,11},{9,10},{10,... | collective-permute-start | bytes 258056 | tf_op jit(solution)/shard_map/ppermute | solution.py:905
  75.3 5.6 %collective-permute-start.10 = (bf16[1,160,384]{2,1,0:T(8,128)(2,1)S(1)}, bf16[1,160,384]{2,1,0:T(8,128)(2,1)S(1)}, u32[]{:S(2)}, u32[]{:S(2)}) collective-permute-start(bf16[1,160,384]{2,1,0:T(8,128)(2,1)S(1)} %get-tuple-element.220), channel_id=1, source_target_pairs={{0,8},{4,12},{8,0},{12,4},{16,24},{20,28},{24,16},{28,20},{1,9},{5... | collective-permute-start | bytes 368648 | tf_op jit(solution)/shard_map/ppermute | solution.py:702
  76.9 7.7 %collective-permute-start.11 = (bf16[1,160,384]{2,1,0:T(8,128)(2,1)S(1)}, bf16[1,160,384]{2,1,0:T(8,128)(2,1)S(1)}, u32[]{:S(2)}, u32[]{:S(2)}) collective-permute-start(bf16[1,160,384]{2,1,0:T(8,128)(2,1)S(1)} %get-tuple-element.222), channel_id=1, source_target_pairs={{0,16},{4,20},{8,24},{12,28},{16,0},{20,4},{24,8},{28,12},{1,17},{... | collective-permute-start | bytes 368648 | tf_op jit(solution)/shard_map/ppermute | solution.py:702
  78.4 6.2 %collective-permute-start.12 = (bf16[1,160,384]{2,1,0:T(8,128)(2,1)S(1)}, bf16[1,160,384]{2,1,0:T(8,128)(2,1)S(1)}, u32[]{:S(2)}, u32[]{:S(2)}) collective-permute-start(bf16[1,160,384]{2,1,0:T(8,128)(2,1)S(1)} %get-tuple-element.221), channel_id=1, source_target_pairs={{0,24},{4,28},{8,16},{12,20},{16,8},{20,12},{24,0},{28,4},{1,25},{... | collective-permute-start | bytes 368648 | tf_op jit(solution)/shard_map/ppermute | solution.py:702
  78.9 5.8 %collective-permute-start.14 = (bf16[112,384]{1,0:T(8,128)(2,1)S(1)}, bf16[112,384]{1,0:T(8,128)(2,1)S(1)}, u32[]{:S(2)}, u32[]{:S(2)}) collective-permute-start(bf16[112,384]{1,0:T(8,128)(2,1)S(1)} %pad_maximum_fusion.3), channel_id=1, source_target_pairs={{0,2},{1,3},{2,0},{3,1},{4,6},{5,7},{6,4},{7,5},{8,10},{9,11},{10,... | collective-permute-start | bytes 258056 | tf_op jit(solution)/shard_map/ppermute | solution.py:905
  80.9 4.6 %collective-permute-start.13 = (bf16[112,384]{1,0:T(8,128)(2,1)S(1)}, bf16[112,384]{1,0:T(8,128)(2,1)S(1)}, u32[]{:S(2)}, u32[]{:S(2)}) collective-permute-start(bf16[112,384]{1,0:T(8,128)(2,1)S(1)} %pad_maximum_fusion.2), channel_id=1, source_target_pairs={{0,1},{1,0},{2,3},{3,2},{4,5},{5,4},{6,7},{7,6},{8,9},{9,8},{10,11... | collective-permute-start | bytes 258056 | tf_op jit(solution)/shard_map/ppermute | solution.py:905
  85.6 6.2 %collective-permute-start.16 = (bf16[176,384]{1,0:T(8,128)(2,1)S(1)}, bf16[176,384]{1,0:T(8,128)(2,1)S(1)}, u32[]{:S(2)}, u32[]{:S(2)}) collective-permute-start(bf16[176,384]{1,0:T(8,128)(2,1)S(1)} %pad_maximum_fusion.1), channel_id=1, source_target_pairs={{0,1},{1,0},{2,3},{3,2},{4,5},{5,4},{6,7},{7,6},{8,9},{9,8},{10,11... | collective-permute-start | bytes 405512 | tf_op jit(solution)/shard_map/ppermute | solution.py:933
  87.1 11.9 %collective-permute-start.17 = (bf16[176,384]{1,0:T(8,128)(2,1)S(1)}, bf16[176,384]{1,0:T(8,128)(2,1)S(1)}, u32[]{:S(2)}, u32[]{:S(2)}) collective-permute-start(bf16[176,384]{1,0:T(8,128)(2,1)S(1)} %pad_maximum_fusion.1), channel_id=1, source_target_pairs={{0,2},{1,3},{2,0},{3,1},{4,6},{5,7},{6,4},{7,5},{8,10},{9,11},{10,... | collective-permute-start | bytes 405512 | tf_op jit(solution)/shard_map/ppermute | solution.py:933
  89.2 9.9 %collective-permute-start.18 = (bf16[176,384]{1,0:T(8,128)(2,1)S(1)}, bf16[176,384]{1,0:T(8,128)(2,1)S(1)}, u32[]{:S(2)}, u32[]{:S(2)}) collective-permute-start(bf16[176,384]{1,0:T(8,128)(2,1)S(1)} %pad_maximum_fusion.1), channel_id=1, source_target_pairs={{0,3},{1,2},{2,1},{3,0},{4,7},{5,6},{6,5},{7,4},{8,11},{9,10},{10,... | collective-permute-start | bytes 405512 | tf_op jit(solution)/shard_map/ppermute | solution.py:933
